TPU v7x, 256 devices: a whole 4x4x8 slice. The times are simulated.
256 devices in a mesh: seq: 32 (over y, x, core), tp: 8 (over z).
Axes of the slice: x: 4, y: 4, z: 8, core: 2. Of those that a mesh axis runs over, the one named last changes fastest.
Arguments:
- query: bfloat16 [32, 16384, 128], P('tp', 'seq'), may hold values from -12 to 12
- keyval: bfloat16 [2, 4, 16384, 128], P(None, None, 'seq'), may hold values from -6 to 6
- vert_blocks: int32 [32, 8], replicated, may hold values from 0 to 255, as said below
- slash_offsets: int32 [32, 8], replicated, may hold values from 0 to 255, as said below
- counts: int32 [32, 2], replicated, may hold values from 1 to 8, as said below
- out_weight: bfloat16 [4096, 8192], P('tp'), may hold values from -0.75 to 0.75
Outputs:
- projected: bfloat16 [16384, 8192], P(('seq', 'tp'))
Inputs may be any that keep to these rules, and one draw needn't show every extreme that they name: `vert_blocks`: the 8 entries of each head's row are distinct; only the first counts[h, 0] are used. `slash_offsets`: the 8 entries of each head's row are distinct and the first is 0; only the first counts[h, 1] are used. `counts`: each column reaches 8 for some head.
All inputs are finite; a program needn't handle non-finite values.
Results may differ from a plain program's by a relative error of at most 0.017.
Values may be sent and summed in bfloat16 or wider, within the bound.
No kernel may reach another device: no remote copies, remote signals or barrier semaphores. Data moves between devices by JAX's collectives and lax.ppermute only.
A program may use at most 128 MiB of HBM per device.

v0:
```python
import functools
import math

import jax
import jax.numpy as jnp
from jax import lax
from jax.experimental import pallas as pl
from jax.experimental.pallas import tpu as pltpu
from jax.sharding import PartitionSpec as P

BLK = 64
NY, NX, NC = 4, 4, 2
DEAD = 1 << 20
SCALE = math.log2(math.e)


def seq_perm(move):
    pairs = []
    for y in range(NY):
        for x in range(NX):
            for c in range(NC):
                ty, tx, tc = move(y, x, c)
                pairs.append(((y * NX + x) * NC + c, ((ty % NY) * NX + tx % NX) * NC + tc))
    return pairs


A_UP = seq_perm(lambda y, x, c: (y, x + 1, c) if c == 0 else (y + 1, x, c))
A_DOWN = seq_perm(lambda y, x, c: (y, x - 1, c) if c == 0 else (y - 1, x, c))
A_FAR = seq_perm(lambda y, x, c: (y, x + 2, c) if c == 0 else (y + 2, x, c))
B_UP = seq_perm(lambda y, x, c: (y + 1, x, c) if c == 0 else (y, x + 1, c))
B_DOWN = seq_perm(lambda y, x, c: (y - 1, x, c) if c == 0 else (y, x - 1, c))
def pair(v, c):
    return (v ^ 1) if c == 0 else (v + 1 if v % 2 else v - 1)


def partner(r, other):
    return seq_perm(
        lambda y, x, c: (
            pair(y, c ^ other) if r & 2 else y,
            pair(x, c ^ other) if r & 1 else x,
            c ^ other,
        )
    )


SWAP = seq_perm(lambda y, x, c: (y, x, 1 - c))


def send(a, pairs):
    return lax.ppermute(a, "seq", pairs)


def shard_slots(seq_index):
    shard = jnp.arange(NY * NX * NC, dtype=jnp.int32)

    def parts(i):
        return i // (NX * NC), (i // NC) % NX, i % NC

    ys, xs, cs = parts(shard)
    y0, x0, c0 = parts(seq_index)
    order = jnp.array([0, 2, 3, 1], jnp.int32)
    in_y, in_x = order[(ys - y0) % NY], order[(xs - x0) % NX]
    first = jnp.where(cs == 0, in_x, in_y)
    second = jnp.where(cs == 0, in_y, in_x)
    return (cs != c0) * 16 + second * 4 + first


def attend_kernel(slots_ref, vert_ref, diag_ref, q_ref, kpv_ref, kpd_ref, *refs):
    pieces, o_ref = refs[:16], refs[16]
    kbuf, vbuf, sv_ref, sd_ref, pv_ref, pd_ref, tot_ref, sems = refs[17:]
    heads, rows, width = q_ref.shape
    blocks = rows // BLK
    per = rows // BLK
    copies = ([], [])
    for side in range(2):
        for which, buf in enumerate((kbuf, vbuf)):
            for j in range(4):
                src = pieces[side * 8 + which * 4 + j]
                copies[which].append(
                    pltpu.make_async_copy(
                        src, buf.at[pl.ds(side * 16 + j * 4, 4)], sems.at[which, side * 4 + j]
                    )
                )
    for c in copies[0] + copies[1]:
        c.start()
    for c in copies[0]:
        c.wait()

    def tile(buf, block):
        return buf[slots_ref[block // per], pl.ds(pl.multiple_of((block % per) * BLK, BLK), BLK), :]

    scale = SCALE / math.sqrt(width)
    nt = (((1,), (1,)), ((), ()))

    def one_head(h, carry):
        verts = [vert_ref[h, c] for c in range(8)]
        diags = [[diag_ref[h * blocks + b, c] for c in range(8)] for b in range(blocks)]
        sv, sd, pv, pd, tot = (r.at[h % 2] for r in (sv_ref, sd_ref, pv_ref, pd_ref, tot_ref))
        k_v = jnp.concatenate([tile(kbuf, v) for v in verts], axis=0)
        sv[...] = lax.dot_general(q_ref[h], k_v, nt, preferred_element_type=jnp.float32)
        for b in range(blocks):
            r = slice(b * BLK, (b + 1) * BLK)
            k_d = jnp.concatenate([tile(kbuf, v) for v in diags[b]], axis=0)
            sd[r, :] = lax.dot_general(q_ref[h, r, :], k_d, nt, preferred_element_type=jnp.float32)
        kpv = kpv_ref[h]
        for b in range(blocks):
            r = slice(b * BLK, (b + 1) * BLK)
            qpos = b * BLK + lax.broadcasted_iota(jnp.int32, (BLK, 1), 0)
            s_d = jnp.where(kpd_ref[h * blocks + b] <= qpos, sd[r, :], -1e30)
            s_v = jnp.where(kpv <= qpos, sv[r, :], -1e30)
            top = jnp.maximum(
                jnp.max(s_d, axis=1, keepdims=True), jnp.max(s_v, axis=1, keepdims=True)
            )
            p_d = jnp.exp2((s_d - top) * scale)
            p_v = jnp.exp2((s_v - top) * scale)
            tot[r, :] = jnp.sum(p_d, axis=1, keepdims=True) + jnp.sum(p_v, axis=1, keepdims=True)
            pv[r, :] = p_v.astype(jnp.bfloat16)
            pd[r, :] = p_d.astype(jnp.bfloat16)

        @pl.when(h == 0)
        def _():
            for c in copies[1]:
                c.wait()

        v_v = jnp.concatenate([tile(vbuf, v) for v in verts], axis=0)
        o_v = jnp.dot(pv[...], v_v, preferred_element_type=jnp.float32)
        for b in range(blocks):
            r = slice(b * BLK, (b + 1) * BLK)
            v_d = jnp.concatenate([tile(vbuf, v) for v in diags[b]], axis=0)
            o_d = jnp.dot(pd[r, :], v_d, preferred_element_type=jnp.float32)
            o = ((o_v[r] + o_d) / tot[r, :]).astype(jnp.bfloat16)
            o_ref[b, :, pl.ds(pl.multiple_of(h * width, width), width)] = o
        return carry

    lax.fori_loop(0, heads, one_head, 0)


def attend(query, pieces, slots, vertical, slash, counts, seq_index):
    heads, rows, width = query.shape
    blocks = rows // BLK
    slot = jnp.arange(8, dtype=jnp.int32)
    first = seq_index * blocks
    vert_live = slot[None, :] < counts[:, 0:1]
    diag = first + jnp.arange(blocks, dtype=jnp.int32)[None, :, None] - slash[:, None, :]
    covered = jnp.any(
        (diag[:, :, :, None] == vertical[:, None, None, :]) & vert_live[:, None, None, :], axis=3
    )
    diag_live = (slot < counts[:, 1:2])[:, None, :] & (diag >= 0) & jnp.logical_not(covered)
    within = jnp.arange(BLK, dtype=jnp.int32)
    kpv = jnp.where(
        vert_live[:, :, None], (vertical - first)[:, :, None] * BLK + within, DEAD
    ).reshape(heads, 1, 8 * BLK)
    kpd = jnp.where(
        diag_live[:, :, :, None], (diag - first)[:, :, :, None] * BLK + within, DEAD
    ).reshape(heads * blocks, 1, 8 * BLK)
    diag = jnp.maximum(diag, 0).reshape(heads * blocks, 8)
    smem = pl.BlockSpec(memory_space=pltpu.SMEM)
    vmem = pl.BlockSpec(memory_space=pltpu.VMEM)
    hbm = pl.BlockSpec(memory_space=pl.ANY)
    f32 = jnp.float32
    return pl.pallas_call(
        attend_kernel,
        out_shape=jax.ShapeDtypeStruct((blocks, BLK, heads * width), jnp.bfloat16),
        in_specs=[smem] * 3 + [vmem] * 3 + [hbm] * len(pieces),
        out_specs=vmem,
        scratch_shapes=[
            pltpu.VMEM((32, rows, width), jnp.bfloat16),
            pltpu.VMEM((32, rows, width), jnp.bfloat16),
            pltpu.VMEM((2, rows, 8 * BLK), f32),
            pltpu.VMEM((2, rows, 8 * BLK), f32),
            pltpu.VMEM((2, rows, 8 * BLK), jnp.bfloat16),
            pltpu.VMEM((2, rows, 8 * BLK), jnp.bfloat16),
            pltpu.VMEM((2, rows, 1), f32),
            pltpu.SemaphoreType.DMA((2, 8)),
        ],
        compiler_params=pltpu.CompilerParams(vmem_limit_bytes=24 * 2**20),
        cost_estimate=pl.CostEstimate(flops=2**31, bytes_accessed=24 * 2**20, transcendentals=2**21),
        name="attend",
    )(slots, vertical, diag, query, kpv, kpd, *pieces)


def ring(n, step):
    return [(i, (i + step) % n) for i in range(n)]


def after(arrays, dep):
    count = len(arrays)
    hbm = pl.BlockSpec(memory_space=pl.ANY)
    return pl.pallas_call(
        lambda *refs: None,
        out_shape=[jax.ShapeDtypeStruct(a.shape, a.dtype) for a in arrays],
        in_specs=[hbm] * (count + 1),
        out_specs=[hbm] * count,
        input_output_aliases={i: i for i in range(count)},
        name="after",
    )(*arrays, dep)


def up(a):
    return lax.ppermute(a, "tp", ring(lax.axis_size("tp"), 1))


def down(a):
    return lax.ppermute(a, "tp", ring(lax.axis_size("tp"), -1))


def project_kernel(steps, last, place_ref, *refs):
    rows, refs = refs[:8], refs[8:]
    count = len(steps)
    parts = 2 if last else 1
    weights, refs = refs[: count * parts], refs[count * parts :]
    if last:
        before, outs, (wbuf, sems) = refs[0], refs[1:9], refs[9:]
    else:
        acc, wbuf, sems = refs
    n, group, depth = rows[0].shape
    tp = place_ref[0]
    copies = [
        pltpu.make_async_copy(
            w, wbuf.at[i // parts, pl.ds((i % parts) * (depth // parts), depth // parts)], sems.at[i]
        )
        for i, w in enumerate(weights)
    ]
    for c in copies:
        c.start()
    def product(i, hops):
        k = lax.rem(tp + hops + n, n)
        a = jnp.concatenate([r[k] for r in rows], axis=0)
        return jnp.dot(a, wbuf[i], preferred_element_type=jnp.float32)

    if last:
        for c in copies:
            c.wait()
        total = before[...] + product(0, steps[0])
        for r, out in enumerate(outs):
            out[...] = total[r * group : (r + 1) * group].astype(jnp.bfloat16)
    else:
        copies[0].wait()
        acc[...] = product(0, 0)

        def add(i, carry):
            pltpu.make_async_copy(wbuf.at[i], wbuf.at[i], sems.at[i]).wait()
            hops = (i + 1) // 2
            acc[...] += product(i, jnp.where(i % 2 == 1, -hops, hops))
            return carry

        lax.fori_loop(1, count, add, 0)


def project(rows, weights, place, steps, before=None):
    n, group, depth = rows[0].shape
    last = before is not None
    cols = weights[0].shape[1]
    vmem = pl.BlockSpec(memory_space=pltpu.VMEM)
    hbm = pl.BlockSpec(memory_space=pltpu.HBM)
    if last:
        shapes = [jax.ShapeDtypeStruct((group, cols), jnp.bfloat16)] * 8
    else:
        shapes = jax.ShapeDtypeStruct((8 * group, cols), jnp.float32)
    return pl.pallas_call(
        functools.partial(project_kernel, steps, last),
        out_shape=shapes,
        in_specs=[pl.BlockSpec(memory_space=pltpu.SMEM)]
        + [vmem] * 8
        + [hbm] * len(weights)
        + [vmem] * last,
        out_specs=[vmem] * 8 if last else vmem,
        scratch_shapes=[
            pltpu.VMEM((len(steps), depth, cols), jnp.bfloat16),
            pltpu.SemaphoreType.DMA((len(weights),)),
        ],
        compiler_params=pltpu.CompilerParams(vmem_limit_bytes=32 * 2**20),
        cost_estimate=pl.CostEstimate(
            flops=2**29 * len(steps), bytes_accessed=2**21 * len(steps), transcendentals=0
        ),
        name="project",
    )(place, *rows, *weights, *([before] if last else []))


def per_device(query, keyval, vert_blocks, slash_offsets, counts, out_weight):
    heads, rows, width = query.shape
    seq_index = lax.axis_index("seq")
    tp_index = lax.axis_index("tp")
    core = seq_index % NC
    x_odd = (seq_index // NC) % 2
    y_odd = (seq_index // (NC * NX)) % 2
    block = y_odd * 2 + x_odd
    cols = out_weight.shape[1] // 8
    depth = out_weight.shape[0] // 2
    kv_head = tp_index // (lax.axis_size("tp") // keyval.shape[1])
    own = lax.dynamic_index_in_dim(keyval, kv_head, 1, keepdims=False)
    w0 = lax.dynamic_slice_in_dim(out_weight, (block * 2 + core) * cols, cols, 1)
    near = [own, send(own, A_UP), send(own, A_DOWN), send(own, A_FAR)]
    w_u1, w_d1 = up(w0), down(w0)
    line_k, line_v = (jnp.stack([a[i] for a in near]) for i in range(2))
    up_k, down_v = send(line_k, B_UP), send(line_v, B_DOWN)
    down_k, up_v = send(line_k, B_DOWN), send(line_v, B_UP)
    far_k, far_v = send(up_k, B_UP), send(down_v, B_DOWN)
    pieces = [line_k, up_k, down_k, far_k, line_v, up_v, down_v, far_v]
    pieces += [send(a, SWAP) for a in pieces]
    w_u1, w_d1 = after([w_u1, w_d1], up_k)
    w_u2, w_d2 = up(w_u1), down(w_d1)

    def mine(a):
        return lax.dynamic_slice_in_dim(a, tp_index * heads, heads, 0)

    attended = attend(
        query, pieces, shard_slots(seq_index), mine(vert_blocks), mine(slash_offsets),
        mine(counts), seq_index,
    )
    w_u2, w_d2 = after([w_u2, w_d2], attended)
    w_u3, w_d3 = up(w_u2), down(w_d2)
    tokens = lax.all_to_all(attended, "tp", split_axis=0, concat_axis=0, tiled=True)
    w_u3, w_d3 = after([w_u3, w_d3], tokens)
    w_u4, w_d4 = up(w_u3[:depth]), down(w_d3[depth:])
    group = [tokens] + [send(tokens, partner(r, 0)) for r in (1, 2, 3)]
    group += [send(a, SWAP) for a in group]
    place = jnp.stack([tp_index, core])
    early = [w0, w_u1, w_d1, w_u2, w_d2, w_u3, w_d3]
    total = project(group, early, place, (0, -1, 1, -2, 2, -3, 3))
    out = project(group, [w_u4, w_d4], place, (4,), total)
    ours = [out[0]] + [send(out[r], partner(r, 0)) for r in (1, 2, 3)]
    theirs = [send(out[r + 4], partner(r, 1)) for r in range(4)]
    first, odd_x, odd_y = core == 0, x_odd == 1, y_odd == 1
    wide = [
        jnp.concatenate([jnp.where(first, a, b), jnp.where(first, b, a)], axis=1)
        for a, b in zip(ours, theirs)
    ]
    wide = [jnp.where(odd_x, wide[i ^ 1], wide[i]) for i in range(4)]
    return jnp.concatenate([jnp.where(odd_y, wide[i ^ 2], wide[i]) for i in range(4)], axis=1)


def solution(mesh):
    return jax.shard_map(
        per_device,
        mesh=mesh,
        in_specs=(P("tp", "seq", None), P(None, None, "seq", None), P(), P(), P(), P("tp", None)),
        out_specs=P(("seq", "tp"), None),
        check_vma=False,
    )
```

profile of v0, /device:TPU:1, one launch (start us, length us, event | category | flops | bytes accessed | tf_op | source)
XLA Modules:
  0.0 148.6 jit_solution(6592699933726391781)
XLA Ops:
  0.0 1.0 dynamic-slice_bitcast_fusion
  1.0 3.8 %collective-permute-start.2 = (bf16[2,512,128]{2,1,0:T(8,128)(2,1)S(1)}, bf16[2,512,128]{2,1,0:T(8,128)(2,1)S(1)}, u32[]{:S(2)}, u32[]{:S(2)}) collective-permute-start(bf16[2,512,128]{2,1,0:T(8,128)(2,1)S(1)} %dynamic-slice_bitcast_fusion), channel_id=1, source_target_pairs={{0,32},{8,136},{16,48},{24,152},{32,0},{40,168},{48,16},{56,184},{... | collective-permute-start | bytes 786440 | tf_op jit(solution)/shard_map/ppermute | solution.py:50
  6.3 1.3 constant_dynamic-slice_fusion.refs_8_
  7.6 5.7 %collective-permute-start.25 = (bf16[512,1024]{1,0:T(8,128)(2,1)S(1)}, bf16[512,1024]{1,0:T(8,128)(2,1)}, u32[]{:S(2)}, u32[]{:S(2)}) collective-permute-start(bf16[512,1024]{1,0:T(8,128)(2,1)S(1)} %constant_dynamic-slice_fusion.refs_8_), channel_id=1, source_target_pairs={{0,7},{1,0},{2,1},{3,2},{4,3},{5,4},{6,5},{7,6},{8,15},{9,8},{10,9... | collective-permute-start | bytes 3145736 | tf_op jit(solution)/shard_map/ppermute | solution.py:204
  13.3 1.0 dynamic-slice_bitcast_fusion.1
  15.2 1.7 %collective-permute-start.9 = (bf16[4,512,128]{2,1,0:T(8,128)(2,1)S(1)}, bf16[4,512,128]{2,1,0:T(8,128)(2,1)}, u32[]{:S(2)}, u32[]{:S(2)}) collective-permute-start(bf16[4,512,128]{2,1,0:T(8,128)(2,1)S(1)} %pad_maximum_fusion.1.refs_0_), channel_id=1, source_target_pairs={{0,8},{8,0},{16,24},{24,16},{32,40},{40,32},{48,56},{56,48},{64,72... | collective-permute-start | bytes 1572872 | tf_op jit(solution)/shard_map/ppermute | solution.py:50
  16.9 2.1 %collective-permute-start.4 = (bf16[4,512,128]{2,1,0:T(8,128)(2,1)S(1)}, bf16[4,512,128]{2,1,0:T(8,128)(2,1)}, u32[]{:S(2)}, u32[]{:S(2)}) collective-permute-start(bf16[4,512,128]{2,1,0:T(8,128)(2,1)S(1)} %pad_maximum_fusion.1.refs_0_), channel_id=1, source_target_pairs={{0,192},{8,56},{16,208},{24,8},{32,224},{40,24},{48,240},{56,40},{... | collective-permute-start | bytes 1572872 | tf_op jit(solution)/shard_map/ppermute | solution.py:50
  19.3 1.0 pad_maximum_fusion.2.refs_4_
  20.4 1.1 collective-permute-start.13
  21.5 3.8 %collective-permute-done.4.refs_2_ = bf16[4,512,128]{2,1,0:T(8,128)(2,1)} collective-permute-done((bf16[4,512,128]{2,1,0:T(8,128)(2,1)S(1)}, bf16[4,512,128]{2,1,0:T(8,128)(2,1)}, u32[]{:S(2)}, u32[]{:S(2)}) %collective-permute-start.4) | collective-permute-done | bytes 524320 | tf_op jit(solution)/shard_map/ppermute | solution.py:50
  25.3 3.3 %collective-permute-start.7 = (bf16[4,512,128]{2,1,0:T(8,128)(2,1)S(1)}, bf16[4,512,128]{2,1,0:T(8,128)(2,1)}, u32[]{:S(2)}, u32[]{:S(2)}) collective-permute-start(bf16[4,512,128]{2,1,0:T(8,128)(2,1)S(1)} %pad_maximum_fusion.2.refs_4_), channel_id=1, source_target_pairs={{0,192},{8,56},{16,208},{24,8},{32,224},{40,24},{48,240},{56,40},{... | collective-permute-start | bytes 1572872 | tf_op jit(solution)/shard_map/ppermute | solution.py:50
  29.7 1.9 %collective-permute-start.11 = (bf16[4,512,128]{2,1,0:T(8,128)(2,1)}, bf16[4,512,128]{2,1,0:T(8,128)(2,1)}, u32[]{:S(2)}, u32[]{:S(2)}) collective-permute-start(bf16[4,512,128]{2,1,0:T(8,128)(2,1)} %collective-permute-done.4.refs_2_), channel_id=1, source_target_pairs={{0,8},{8,0},{16,24},{24,16},{32,40},{40,32},{48,56},{56,48},{64,72... | collective-permute-start | bytes 1572872 | tf_op jit(solution)/shard_map/ppermute | solution.py:50
  31.5 3.2 %collective-permute-done.7.refs_6_ = bf16[4,512,128]{2,1,0:T(8,128)(2,1)} collective-permute-done((bf16[4,512,128]{2,1,0:T(8,128)(2,1)S(1)}, bf16[4,512,128]{2,1,0:T(8,128)(2,1)}, u32[]{:S(2)}, u32[]{:S(2)}) %collective-permute-start.7) | collective-permute-done | bytes 524320 | tf_op jit(solution)/shard_map/ppermute | solution.py:50
  34.7 2.5 %collective-permute-start.10 = (bf16[4,512,128]{2,1,0:T(8,128)(2,1)S(1)}, bf16[4,512,128]{2,1,0:T(8,128)(2,1)}, u32[]{:S(2)}, u32[]{:S(2)}) collective-permute-start(bf16[4,512,128]{2,1,0:T(8,128)(2,1)S(1)} %collective-permute-done.3.refs_1_.refs_2_), channel_id=1, source_target_pairs={{0,8},{8,0},{16,24},{24,16},{32,40},{40,32},{48,56},{56,48},{64,72... | collective-permute-start | bytes 1572872 | tf_op jit(solution)/shard_map/ppermute | solution.py:50
  38.3 2.7 %collective-permute-start.15 = (bf16[4,512,128]{2,1,0:T(8,128)(2,1)}, bf16[4,512,128]{2,1,0:T(8,128)(2,1)}, u32[]{:S(2)}, u32[]{:S(2)}) collective-permute-start(bf16[4,512,128]{2,1,0:T(8,128)(2,1)} %collective-permute-done.7.refs_6_), channel_id=1, source_target_pairs={{0,8},{8,0},{16,24},{24,16},{32,40},{40,32},{48,56},{56,48},{64,72... | collective-permute-start | bytes 1572872 | tf_op jit(solution)/shard_map/ppermute | solution.py:50
  41.1 2.1 %collective-permute-start.8 = (bf16[4,512,128]{2,1,0:T(8,128)(2,1)}, bf16[4,512,128]{2,1,0:T(8,128)(2,1)}, u32[]{:S(2)}, u32[]{:S(2)}) collective-permute-start(bf16[4,512,128]{2,1,0:T(8,128)(2,1)} %collective-permute-done.7.refs_6_), channel_id=1, source_target_pairs={{0,192},{8,56},{16,208},{24,8},{32,224},{40,24},{48,240},{56,40},{... | collective-permute-start | bytes 1572872 | tf_op jit(solution)/shard_map/ppermute | solution.py:50
  43.7 3.3 %collective-permute-start.27 = (bf16[512,1024]{1,0:T(8,128)(2,1)}, bf16[512,1024]{1,0:T(8,128)(2,1)}, u32[]{:S(2)}, u32[]{:S(2)}) collective-permute-start(bf16[512,1024]{1,0:T(8,128)(2,1)} %get-tuple-element.20.refs_10_), channel_id=1, source_target_pairs={{0,7},{1,0},{2,1},{3,2},{4,3},{5,4},{6,5},{7,6},{8,15},{9,8},{10,9... | collective-permute-start | bytes 3145736 | tf_op jit(solution)/shard_map/ppermute | solution.py:204
  48.0 3.5 %collective-permute-start.14 = (bf16[4,512,128]{2,1,0:T(8,128)(2,1)}, bf16[4,512,128]{2,1,0:T(8,128)(2,1)S(1)}, u32[]{:S(2)}, u32[]{:S(2)}) collective-permute-start(bf16[4,512,128]{2,1,0:T(8,128)(2,1)} %copy-done.16), channel_id=1, source_target_pairs={{0,8},{8,0},{16,24},{24,16},{32,40},{40,32},{48,56},{56,48},{64,72... | collective-permute-start | bytes 1572872 | tf_op jit(solution)/shard_map/ppermute | solution.py:50
  52.2 1.1 collective-permute-done.14.refs_13_
  54.7 1.0 copy-done.8
  55.8 1.0 copy-done.15
  56.8 1.0 copy-done.17
  57.8 9.6 %attend.1.refs_2_ = bf16[8,64,512]{2,1,0:T(8,128)(2,1)} custom-call(s32[32]{0:T(128)S(1)} %fusion.4.slots_ref, s32[4,8]{1,0:T(4,128)S(1)} %copy.24.vert_ref, s32[32,8]{1,0:T(8,128)S(1)} %fusion.diag_ref, bf16[4,512,128]{2,1,0:T(8,128)(2,1)S(1)} %copy-done.13, s32[4,1,512]{2,1,0:T(1,128)S(1)} %add_select_fusion.1.kpv_ref, ...), custom_call_target="tpu_custom_call" | custom-call | flops 2147483648 | bytes 25165824 | tf_op jit(solution)/shard_map/attend/pallas_call | solution.py:161
  67.4 6.5 %all-to-all-start = ((bf16[8,64,512]{2,1,0:T(8,128)(2,1)}), bf16[8,64,512]{2,1,0:T(8,128)(2,1)S(1)}, u32[]{:S(2)}, u32[]{:S(2)}) async-start(bf16[8,64,512]{2,1,0:T(8,128)(2,1)} %attend.1.refs_2_), calls=%async_computation | async-start | bytes 1048576 | tf_op jit(solution)/shard_map/all_to_all | solution.py:313
  74.9 1.5 collective-permute-start.28
  76.4 1.2 collective-permute-start.29
  77.6 14.1 %all-to-all-done.refs_2_.refs_0_ = bf16[8,64,512]{2,1,0:T(8,128)(2,1)S(1)} async-done(((bf16[8,64,512]{2,1,0:T(8,128)(2,1)}), bf16[8,64,512]{2,1,0:T(8,128)(2,1)S(1)}, u32[]{:S(2)}, u32[]{:S(2)}) %all-to-all-start) | async-done | bytes 524320 | tf_op jit(solution)/shard_map/all_to_all | solution.py:313
  91.7 2.9 %collective-permute-start.19 = (bf16[8,64,512]{2,1,0:T(8,128)(2,1)S(1)}, bf16[8,64,512]{2,1,0:T(8,128)(2,1)S(1)}, u32[]{:S(2)}, u32[]{:S(2)}) collective-permute-start(bf16[8,64,512]{2,1,0:T(8,128)(2,1)S(1)} %all-to-all-done.refs_2_.refs_0_), channel_id=1, source_target_pairs={{0,80},{8,248},{16,64},{24,232},{32,112},{40,216},{48,96},{56,200}... | collective-permute-start | bytes 1572872 | tf_op jit(solution)/shard_map/ppermute | solution.py:50
  95.5 1.3 collective-permute-start.17
  96.8 14.0 %collective-permute-done.28.refs_0_ = bf16[512,1024]{1,0:T(8,128)(2,1)S(1)} collective-permute-done((bf16[512,1024]{1,0:T(8,128)(2,1)}, bf16[512,1024]{1,0:T(8,128)(2,1)S(1)}, u32[]{:S(2)}, u32[]{:S(2)}) %collective-permute-start.28) | collective-permute-done | bytes 1048608 | tf_op jit(solution)/shard_map/ppermute | solution.py:200
  110.7 1.4 collective-permute-start.20
  112.8 1.0 copy-done.5
  113.8 1.2 slice.58
  115.0 1.1 slice.57
  116.2 2.7 %collective-permute-start.31 = (bf16[256,1024]{1,0:T(8,128)(2,1)S(1)}, bf16[256,1024]{1,0:T(8,128)(2,1)S(1)}, u32[]{:S(2)}, u32[]{:S(2)}) collective-permute-start(bf16[256,1024]{1,0:T(8,128)(2,1)S(1)} %slice.58), channel_id=1, source_target_pairs={{0,7},{1,0},{2,1},{3,2},{4,3},{5,4},{6,5},{7,6},{8,15},{9,8},{10,9... | collective-permute-start | bytes 1572872 | tf_op jit(solution)/shard_map/ppermute | solution.py:204
  118.9 1.2 copy-done.6
  120.2 1.2 copy-done.10
  121.4 1.2 copy-done.12
  122.6 7.6 %project.2.refs_10_ = f32[512,1024]{1,0:T(8,128)S(1)} custom-call(s32[2]{0:T(128)S(1)} %pad_add_fusion.place_ref, bf16[8,64,512]{2,1,0:T(8,128)(2,1)S(1)} %copy-done.2, bf16[8,64,512]{2,1,0:T(8,128)(2,1)} %collective-permute-done.17.refs_1_, bf16[8,64,512]{2,1,0:T(8,128)(2,1)} %collective-permute-done.18.refs_2_, ...), custom_call_target="tpu_custom_call" | custom-call | flops 3758096384 | bytes 14680064 | tf_op jit(solution)/shard_map/project/pallas_call | solution.py:260
  130.4 2.7 %project.3 = (bf16[64,1024]{1,0:T(8,128)(2,1)S(1)}, bf16[64,1024]{1,0:T(8,128)(2,1)S(1)}, bf16[64,1024]{1,0:T(8,128)(2,1)S(1)}, bf16[64,1024]{1,0:T(8,128)(2,1)S...) custom-call(s32[2]{0:T(128)S(1)} %pad_add_fusion.place_ref, ...), custom_call_target="tpu_custom_call" | custom-call | flops 536870912 | bytes 2097152 | tf_op jit(solution)/shard_map/project/pallas_call | solution.py:260
  133.1 3.0 %collective-permute-start.32 = (bf16[64,1024]{1,0:T(8,128)(2,1)S(1)}, bf16[64,1024]{1,0:T(8,128)(2,1)S(1)}, u32[]{:S(2)}, u32[]{:S(2)}) collective-permute-start(bf16[64,1024]{1,0:T(8,128)(2,1)S(1)} %get-tuple-element.25), channel_id=1, source_target_pairs={{0,80},{8,248},{16,64},{24,232},{32,112},{40,216},{48,96},{56,200}... | collective-permute-start | bytes 393224 | tf_op jit(solution)/shard_map/ppermute | solution.py:50
  137.0 1.8 %collective-permute-start.34 = (bf16[64,1024]{1,0:T(8,128)(2,1)S(1)}, bf16[64,1024]{1,0:T(8,128)(2,1)S(1)}, u32[]{:S(2)}, u32[]{:S(2)}) collective-permute-start(bf16[64,1024]{1,0:T(8,128)(2,1)S(1)} %get-tuple-element.27), channel_id=1, source_target_pairs={{0,64},{8,200},{16,80},{24,216},{32,96},{40,232},{48,112},{56,248}... | collective-permute-start | bytes 393224 | tf_op jit(solution)/shard_map/ppermute | solution.py:50
  138.7 1.3 collective-permute-start.35
  140.0 1.4 collective-permute-start.36
  141.7 2.2 %collective-permute-done.33 = bf16[64,1024]{1,0:T(8,128)(2,1)S(1)} collective-permute-done((bf16[64,1024]{1,0:T(8,128)(2,1)S(1)}, bf16[64,1024]{1,0:T(8,128)(2,1)S(1)}, u32[]{:S(2)}, u32[]{:S(2)}) %collective-permute-start.33) | collective-permute-done | bytes 131104 | tf_op jit(solution)/shard_map/ppermute | solution.py:50
  144.0 1.3 collective-permute-done.35
  145.3 1.8 %collective-permute-done.37 = bf16[64,1024]{1,0:T(8,128)(2,1)S(1)} collective-permute-done((bf16[64,1024]{1,0:T(8,128)(2,1)S(1)}, bf16[64,1024]{1,0:T(8,128)(2,1)S(1)}, u32[]{:S(2)}, u32[]{:S(2)}) %collective-permute-start.37) | collective-permute-done | bytes 131104 | tf_op jit(solution)/shard_map/ppermute | solution.py:50
  147.5 1.0 pad_maximum_fusion
  (124 shorter events, 13.0 us)
Async XLA Ops:
  0.0 14.3 %copy-start = (s32[32,8]{0,1:T(8,128)S(1)}, s32[32,8]{0,1:T(8,128)}, u32[]{:S(2)}) copy-start(s32[32,8]{0,1:T(8,128)} %param.9) | copy-start | bytes 3076
  1.0 13.4 %collective-permute-start.2 = (bf16[2,512,128]{2,1,0:T(8,128)(2,1)S(1)}, bf16[2,512,128]{2,1,0:T(8,128)(2,1)S(1)}, u32[]{:S(2)}, u32[]{:S(2)}) collective-permute-start(bf16[2,512,128]{2,1,0:T(8,128)(2,1)S(1)} %dynamic-slice_bitcast_fusion), channel_id=1, source_target_pairs={{0,32},{8,136},{16,48},{24,152},{32,0},{40,168},{48,16},{56,184},{... | collective-permute-start | bytes 786440 | tf_op jit(solution)/shard_map/ppermute | solution.py:50
  4.8 9.6 %collective-permute-start.1 = (bf16[2,512,128]{2,1,0:T(8,128)(2,1)S(1)}, bf16[2,512,128]{2,1,0:T(8,128)(2,1)S(1)}, u32[]{:S(2)}, u32[]{:S(2)}) collective-permute-start(bf16[2,512,128]{2,1,0:T(8,128)(2,1)S(1)} %dynamic-slice_bitcast_fusion), channel_id=1, source_target_pairs={{0,48},{8,200},{16,0},{24,216},{32,16},{40,232},{48,32},{56,248},{... | collective-permute-start | bytes 786440 | tf_op jit(solution)/shard_map/ppermute | solution.py:50
  5.6 8.8 %collective-permute-start = (bf16[2,512,128]{2,1,0:T(8,128)(2,1)S(1)}, bf16[2,512,128]{2,1,0:T(8,128)(2,1)S(1)}, u32[]{:S(2)}, u32[]{:S(2)}) collective-permute-start(bf16[2,512,128]{2,1,0:T(8,128)(2,1)S(1)} %dynamic-slice_bitcast_fusion), channel_id=1, source_target_pairs={{0,16},{8,72},{16,32},{24,88},{32,48},{40,104},{48,0},{56,120},{64... | collective-permute-start | bytes 786440 | tf_op jit(solution)/shard_map/ppermute | solution.py:50
  7.6 12.8 %copy-start.9 = (bf16[512,1024]{1,0:T(8,128)(2,1)}, bf16[512,1024]{1,0:T(8,128)(2,1)S(1)}, u32[]{:S(2)}) copy-start(bf16[512,1024]{1,0:T(8,128)(2,1)S(1)} %constant_dynamic-slice_fusion.refs_8_) | copy-start | bytes 3145732
  7.6 11.4 %copy-start.18 = (s32[32,8]{0,1:T(8,128)S(1)}, s32[32,8]{0,1:T(8,128)}, u32[]{:S(2)}) copy-start(s32[32,8]{0,1:T(8,128)} %param.10) | copy-start | bytes 3076
  7.6 11.5 %copy-start.19 = (s32[32,2]{0,1:T(2,128)S(1)}, s32[32,2]{0,1:T(2,128)}, u32[]{:S(2)}) copy-start(s32[32,2]{0,1:T(2,128)} %param.11) | copy-start | bytes 772
  7.6 30.7 %collective-permute-start.25 = (bf16[512,1024]{1,0:T(8,128)(2,1)S(1)}, bf16[512,1024]{1,0:T(8,128)(2,1)}, u32[]{:S(2)}, u32[]{:S(2)}) collective-permute-start(bf16[512,1024]{1,0:T(8,128)(2,1)S(1)} %constant_dynamic-slice_fusion.refs_8_), channel_id=1, source_target_pairs={{0,7},{1,0},{2,1},{3,2},{4,3},{5,4},{6,5},{7,6},{8,15},{9,8},{10,9... | collective-permute-start | bytes 3145736 | tf_op jit(solution)/shard_map/ppermute | solution.py:204
  13.3 27.8 %collective-permute-start.24 = (bf16[512,1024]{1,0:T(8,128)(2,1)S(1)}, bf16[512,1024]{1,0:T(8,128)(2,1)}, u32[]{:S(2)}, u32[]{:S(2)}) collective-permute-start(bf16[512,1024]{1,0:T(8,128)(2,1)S(1)} %constant_dynamic-slice_fusion.refs_8_), channel_id=1, source_target_pairs={{0,1},{1,2},{2,3},{3,4},{4,5},{5,6},{6,7},{7,0},{8,9},{9,10},{10,1... | collective-permute-start | bytes 3145736 | tf_op jit(solution)/shard_map/ppermute | solution.py:200
  15.2 5.2 %collective-permute-start.9 = (bf16[4,512,128]{2,1,0:T(8,128)(2,1)S(1)}, bf16[4,512,128]{2,1,0:T(8,128)(2,1)}, u32[]{:S(2)}, u32[]{:S(2)}) collective-permute-start(bf16[4,512,128]{2,1,0:T(8,128)(2,1)S(1)} %pad_maximum_fusion.1.refs_0_), channel_id=1, source_target_pairs={{0,8},{8,0},{16,24},{24,16},{32,40},{40,32},{48,56},{56,48},{64,72... | collective-permute-start | bytes 1572872 | tf_op jit(solution)/shard_map/ppermute | solution.py:50
  16.9 8.4 %collective-permute-start.4 = (bf16[4,512,128]{2,1,0:T(8,128)(2,1)S(1)}, bf16[4,512,128]{2,1,0:T(8,128)(2,1)}, u32[]{:S(2)}, u32[]{:S(2)}) collective-permute-start(bf16[4,512,128]{2,1,0:T(8,128)(2,1)S(1)} %pad_maximum_fusion.1.refs_0_), channel_id=1, source_target_pairs={{0,192},{8,56},{16,208},{24,8},{32,224},{40,24},{48,240},{56,40},{... | collective-permute-start | bytes 1572872 | tf_op jit(solution)/shard_map/ppermute | solution.py:50
  19.0 9.7 %collective-permute-start.3 = (bf16[4,512,128]{2,1,0:T(8,128)(2,1)S(1)}, bf16[4,512,128]{2,1,0:T(8,128)(2,1)S(1)}, u32[]{:S(2)}, u32[]{:S(2)}) collective-permute-start(bf16[4,512,128]{2,1,0:T(8,128)(2,1)S(1)} %pad_maximum_fusion.1.refs_0_), channel_id=1, source_target_pairs={{0,64},{8,24},{16,80},{24,40},{32,96},{40,56},{48,112},{56,8},{64,... | collective-permute-start | bytes 1572872 | tf_op jit(solution)/shard_map/ppermute | solution.py:50
  19.3 35.4 %copy-start.13 = (bf16[4,512,128]{2,1,0:T(8,128)(2,1)S(1)}, bf16[4,512,128]{2,1,0:T(8,128)(2,1)}, u32[]{:S(2)}) copy-start(bf16[4,512,128]{2,1,0:T(8,128)(2,1)} %q_ref.1) | copy-start | bytes 1572868
  20.4 8.5 %collective-permute-start.13 = (bf16[4,512,128]{2,1,0:T(8,128)(2,1)S(1)}, bf16[4,512,128]{2,1,0:T(8,128)(2,1)S(1)}, u32[]{:S(2)}, u32[]{:S(2)}) collective-permute-start(bf16[4,512,128]{2,1,0:T(8,128)(2,1)S(1)} %pad_maximum_fusion.2.refs_4_), channel_id=1, source_target_pairs={{0,8},{8,0},{16,24},{24,16},{32,40},{40,32},{48,56},{56,48},{64,72... | collective-permute-start | bytes 1572872 | tf_op jit(solution)/shard_map/ppermute | solution.py:50
  25.3 9.4 %collective-permute-start.7 = (bf16[4,512,128]{2,1,0:T(8,128)(2,1)S(1)}, bf16[4,512,128]{2,1,0:T(8,128)(2,1)}, u32[]{:S(2)}, u32[]{:S(2)}) collective-permute-start(bf16[4,512,128]{2,1,0:T(8,128)(2,1)S(1)} %pad_maximum_fusion.2.refs_4_), channel_id=1, source_target_pairs={{0,192},{8,56},{16,208},{24,8},{32,224},{40,24},{48,240},{56,40},{... | collective-permute-start | bytes 1572872 | tf_op jit(solution)/shard_map/ppermute | solution.py:50
  28.7 14.7 %copy-start.7 = (bf16[4,512,128]{2,1,0:T(8,128)(2,1)}, bf16[4,512,128]{2,1,0:T(8,128)(2,1)S(1)}, u32[]{:S(2)}) copy-start(bf16[4,512,128]{2,1,0:T(8,128)(2,1)S(1)} %collective-permute-done.3.refs_1_.refs_2_) | copy-start | bytes 1572868
  28.7 9.6 %collective-permute-start.6 = (bf16[4,512,128]{2,1,0:T(8,128)(2,1)S(1)}, bf16[4,512,128]{2,1,0:T(8,128)(2,1)S(1)}, u32[]{:S(2)}, u32[]{:S(2)}) collective-permute-start(bf16[4,512,128]{2,1,0:T(8,128)(2,1)S(1)} %pad_maximum_fusion.2.refs_4_), channel_id=1, source_target_pairs={{0,64},{8,24},{16,80},{24,40},{32,96},{40,56},{48,112},{56,8},{64,... | collective-permute-start | bytes 1572872 | tf_op jit(solution)/shard_map/ppermute | solution.py:50
  29.7 13.7 %collective-permute-start.11 = (bf16[4,512,128]{2,1,0:T(8,128)(2,1)}, bf16[4,512,128]{2,1,0:T(8,128)(2,1)}, u32[]{:S(2)}, u32[]{:S(2)}) collective-permute-start(bf16[4,512,128]{2,1,0:T(8,128)(2,1)} %collective-permute-done.4.refs_2_), channel_id=1, source_target_pairs={{0,8},{8,0},{16,24},{24,16},{32,40},{40,32},{48,56},{56,48},{64,72... | collective-permute-start | bytes 1572872 | tf_op jit(solution)/shard_map/ppermute | solution.py:50
  34.7 8.9 %collective-permute-start.10 = (bf16[4,512,128]{2,1,0:T(8,128)(2,1)S(1)}, bf16[4,512,128]{2,1,0:T(8,128)(2,1)}, u32[]{:S(2)}, u32[]{:S(2)}) collective-permute-start(bf16[4,512,128]{2,1,0:T(8,128)(2,1)S(1)} %collective-permute-done.3.refs_1_.refs_2_), channel_id=1, source_target_pairs={{0,8},{8,0},{16,24},{24,16},{32,40},{40,32},{48,56},{56,48},{64,72... | collective-permute-start | bytes 1572872 | tf_op jit(solution)/shard_map/ppermute | solution.py:50
  38.3 9.6 %collective-permute-start.5 = (bf16[4,512,128]{2,1,0:T(8,128)(2,1)S(1)}, bf16[4,512,128]{2,1,0:T(8,128)(2,1)}, u32[]{:S(2)}, u32[]{:S(2)}) collective-permute-start(bf16[4,512,128]{2,1,0:T(8,128)(2,1)S(1)} %collective-permute-done.3.refs_1_.refs_2_), channel_id=1, source_target_pairs={{0,64},{8,24},{16,80},{24,40},{32,96},{40,56},{48,112},{56,8},{64,... | collective-permute-start | bytes 1572872 | tf_op jit(solution)/shard_map/ppermute | solution.py:50
  38.3 13.1 %collective-permute-start.15 = (bf16[4,512,128]{2,1,0:T(8,128)(2,1)}, bf16[4,512,128]{2,1,0:T(8,128)(2,1)}, u32[]{:S(2)}, u32[]{:S(2)}) collective-permute-start(bf16[4,512,128]{2,1,0:T(8,128)(2,1)} %collective-permute-done.7.refs_6_), channel_id=1, source_target_pairs={{0,8},{8,0},{16,24},{24,16},{32,40},{40,32},{48,56},{56,48},{64,72... | collective-permute-start | bytes 1572872 | tf_op jit(solution)/shard_map/ppermute | solution.py:50
  41.1 10.4 %collective-permute-start.8 = (bf16[4,512,128]{2,1,0:T(8,128)(2,1)}, bf16[4,512,128]{2,1,0:T(8,128)(2,1)}, u32[]{:S(2)}, u32[]{:S(2)}) collective-permute-start(bf16[4,512,128]{2,1,0:T(8,128)(2,1)} %collective-permute-done.7.refs_6_), channel_id=1, source_target_pairs={{0,192},{8,56},{16,208},{24,8},{32,224},{40,24},{48,240},{56,40},{... | collective-permute-start | bytes 1572872 | tf_op jit(solution)/shard_map/ppermute | solution.py:50
  43.4 30.5 %collective-permute-start.26 = (bf16[512,1024]{1,0:T(8,128)(2,1)}, bf16[512,1024]{1,0:T(8,128)(2,1)S(1)}, u32[]{:S(2)}, u32[]{:S(2)}) collective-permute-start(bf16[512,1024]{1,0:T(8,128)(2,1)} %get-tuple-element.19.refs_9_), channel_id=1, source_target_pairs={{0,1},{1,2},{2,3},{3,4},{4,5},{5,6},{6,7},{7,0},{8,9},{9,10},{10,1... | collective-permute-start | bytes 3145736 | tf_op jit(solution)/shard_map/ppermute | solution.py:200
  43.7 30.3 %collective-permute-start.27 = (bf16[512,1024]{1,0:T(8,128)(2,1)}, bf16[512,1024]{1,0:T(8,128)(2,1)}, u32[]{:S(2)}, u32[]{:S(2)}) collective-permute-start(bf16[512,1024]{1,0:T(8,128)(2,1)} %get-tuple-element.20.refs_10_), channel_id=1, source_target_pairs={{0,7},{1,0},{2,1},{3,2},{4,3},{5,4},{6,5},{7,6},{8,15},{9,8},{10,9... | collective-permute-start | bytes 3145736 | tf_op jit(solution)/shard_map/ppermute | solution.py:204
  48.0 5.2 %collective-permute-start.14 = (bf16[4,512,128]{2,1,0:T(8,128)(2,1)}, bf16[4,512,128]{2,1,0:T(8,128)(2,1)S(1)}, u32[]{:S(2)}, u32[]{:S(2)}) collective-permute-start(bf16[4,512,128]{2,1,0:T(8,128)(2,1)} %copy-done.16), channel_id=1, source_target_pairs={{0,8},{8,0},{16,24},{24,16},{32,40},{40,32},{48,56},{56,48},{64,72... | collective-permute-start | bytes 1572872 | tf_op jit(solution)/shard_map/ppermute | solution.py:50
  51.5 2.5 %collective-permute-start.12 = (bf16[4,512,128]{2,1,0:T(8,128)(2,1)}, bf16[4,512,128]{2,1,0:T(8,128)(2,1)S(1)}, u32[]{:S(2)}, u32[]{:S(2)}) collective-permute-start(bf16[4,512,128]{2,1,0:T(8,128)(2,1)} %collective-permute-done.5.refs_3_), channel_id=1, source_target_pairs={{0,8},{8,0},{16,24},{24,16},{32,40},{40,32},{48,56},{56,48},{64,72... | collective-permute-start | bytes 1572872 | tf_op jit(solution)/shard_map/ppermute | solution.py:50
  51.5 3.2 %collective-permute-start.16 = (bf16[4,512,128]{2,1,0:T(8,128)(2,1)}, bf16[4,512,128]{2,1,0:T(8,128)(2,1)S(1)}, u32[]{:S(2)}, u32[]{:S(2)}) collective-permute-start(bf16[4,512,128]{2,1,0:T(8,128)(2,1)} %collective-permute-done.8.refs_7_), channel_id=1, source_target_pairs={{0,8},{8,0},{16,24},{24,16},{32,40},{40,32},{48,56},{56,48},{64,72... | collective-permute-start | bytes 1572872 | tf_op jit(solution)/shard_map/ppermute | solution.py:50
  67.4 24.3 %all-to-all-start = ((bf16[8,64,512]{2,1,0:T(8,128)(2,1)}), bf16[8,64,512]{2,1,0:T(8,128)(2,1)S(1)}, u32[]{:S(2)}, u32[]{:S(2)}) async-start(bf16[8,64,512]{2,1,0:T(8,128)(2,1)} %attend.1.refs_2_), calls=%async_computation | async-start | bytes 1048576 | tf_op jit(solution)/shard_map/all_to_all | solution.py:313
  74.9 35.8 %collective-permute-start.28 = (bf16[512,1024]{1,0:T(8,128)(2,1)}, bf16[512,1024]{1,0:T(8,128)(2,1)S(1)}, u32[]{:S(2)}, u32[]{:S(2)}) collective-permute-start(bf16[512,1024]{1,0:T(8,128)(2,1)} %get-tuple-element.21.refs_11_), channel_id=1, source_target_pairs={{0,1},{1,2},{2,3},{3,4},{4,5},{5,6},{6,7},{7,0},{8,9},{9,10},{10,1... | collective-permute-start | bytes 3145736 | tf_op jit(solution)/shard_map/ppermute | solution.py:200
  76.4 36.4 %collective-permute-start.29 = (bf16[512,1024]{1,0:T(8,128)(2,1)}, bf16[512,1024]{1,0:T(8,128)(2,1)S(1)}, u32[]{:S(2)}, u32[]{:S(2)}) collective-permute-start(bf16[512,1024]{1,0:T(8,128)(2,1)} %get-tuple-element.22.refs_12_), channel_id=1, source_target_pairs={{0,7},{1,0},{2,1},{3,2},{4,3},{5,4},{6,5},{7,6},{8,15},{9,8},{10,9... | collective-permute-start | bytes 3145736 | tf_op jit(solution)/shard_map/ppermute | solution.py:204
  91.7 21.1 %copy-start.1 = (bf16[8,64,512]{2,1,0:T(8,128)(2,1)}, bf16[8,64,512]{2,1,0:T(8,128)(2,1)S(1)}, u32[]{:S(2)}) copy-start(bf16[8,64,512]{2,1,0:T(8,128)(2,1)S(1)} %all-to-all-done.refs_2_.refs_0_) | copy-start | bytes 1572868
  91.7 20.4 %collective-permute-start.19 = (bf16[8,64,512]{2,1,0:T(8,128)(2,1)S(1)}, bf16[8,64,512]{2,1,0:T(8,128)(2,1)S(1)}, u32[]{:S(2)}, u32[]{:S(2)}) collective-permute-start(bf16[8,64,512]{2,1,0:T(8,128)(2,1)S(1)} %all-to-all-done.refs_2_.refs_0_), channel_id=1, source_target_pairs={{0,80},{8,248},{16,64},{24,232},{32,112},{40,216},{48,96},{56,200}... | collective-permute-start | bytes 1572872 | tf_op jit(solution)/shard_map/ppermute | solution.py:50
  94.6 17.6 %collective-permute-start.18 = (bf16[8,64,512]{2,1,0:T(8,128)(2,1)S(1)}, bf16[8,64,512]{2,1,0:T(8,128)(2,1)}, u32[]{:S(2)}, u32[]{:S(2)}) collective-permute-start(bf16[8,64,512]{2,1,0:T(8,128)(2,1)S(1)} %all-to-all-done.refs_2_.refs_0_), channel_id=1, source_target_pairs={{0,64},{8,200},{16,80},{24,216},{32,96},{40,232},{48,112},{56,248}... | collective-permute-start | bytes 1572872 | tf_op jit(solution)/shard_map/ppermute | solution.py:50
  95.5 17.1 %collective-permute-start.17 = (bf16[8,64,512]{2,1,0:T(8,128)(2,1)S(1)}, bf16[8,64,512]{2,1,0:T(8,128)(2,1)}, u32[]{:S(2)}, u32[]{:S(2)}) collective-permute-start(bf16[8,64,512]{2,1,0:T(8,128)(2,1)S(1)} %all-to-all-done.refs_2_.refs_0_), channel_id=1, source_target_pairs={{0,16},{8,56},{16,0},{24,40},{32,48},{40,24},{48,32},{56,8},{64,80... | collective-permute-start | bytes 1572872 | tf_op jit(solution)/shard_map/ppermute | solution.py:50
  110.7 5.4 %collective-permute-start.20 = (bf16[8,64,512]{2,1,0:T(8,128)(2,1)S(1)}, bf16[8,64,512]{2,1,0:T(8,128)(2,1)}, u32[]{:S(2)}, u32[]{:S(2)}) collective-permute-start(bf16[8,64,512]{2,1,0:T(8,128)(2,1)S(1)} %all-to-all-done.refs_2_.refs_0_), channel_id=1, source_target_pairs={{0,8},{8,0},{16,24},{24,16},{32,40},{40,32},{48,56},{56,48},{64,72... | collective-permute-start | bytes 1572872 | tf_op jit(solution)/shard_map/ppermute | solution.py:50
  112.2 6.7 %collective-permute-start.23 = (bf16[8,64,512]{2,1,0:T(8,128)(2,1)S(1)}, bf16[8,64,512]{2,1,0:T(8,128)(2,1)}, u32[]{:S(2)}, u32[]{:S(2)}) collective-permute-start(bf16[8,64,512]{2,1,0:T(8,128)(2,1)S(1)} %collective-permute-done.19.refs_3_), channel_id=1, source_target_pairs={{0,8},{8,0},{16,24},{24,16},{32,40},{40,32},{48,56},{56,48},{64,72... | collective-permute-start | bytes 1572872 | tf_op jit(solution)/shard_map/ppermute | solution.py:50
  112.3 6.6 %collective-permute-start.22 = (bf16[8,64,512]{2,1,0:T(8,128)(2,1)}, bf16[8,64,512]{2,1,0:T(8,128)(2,1)}, u32[]{:S(2)}, u32[]{:S(2)}) collective-permute-start(bf16[8,64,512]{2,1,0:T(8,128)(2,1)} %collective-permute-done.18.refs_2_), channel_id=1, source_target_pairs={{0,8},{8,0},{16,24},{24,16},{32,40},{40,32},{48,56},{56,48},{64,72... | collective-permute-start | bytes 1572872 | tf_op jit(solution)/shard_map/ppermute | solution.py:50
  112.7 6.2 %collective-permute-start.21 = (bf16[8,64,512]{2,1,0:T(8,128)(2,1)}, bf16[8,64,512]{2,1,0:T(8,128)(2,1)}, u32[]{:S(2)}, u32[]{:S(2)}) collective-permute-start(bf16[8,64,512]{2,1,0:T(8,128)(2,1)} %collective-permute-done.17.refs_1_), channel_id=1, source_target_pairs={{0,8},{8,0},{16,24},{24,16},{32,40},{40,32},{48,56},{56,48},{64,72... | collective-permute-start | bytes 1572872 | tf_op jit(solution)/shard_map/ppermute | solution.py:50
  113.8 5.1 %copy-start.4 = (bf16[512,1024]{1,0:T(8,128)(2,1)S(1)}, bf16[512,1024]{1,0:T(8,128)(2,1)}, u32[]{:S(2)}) copy-start(bf16[512,1024]{1,0:T(8,128)(2,1)} %get-tuple-element.23.refs_13_) | copy-start | bytes 3145732
  116.1 14.4 %collective-permute-start.30 = (bf16[256,1024]{1,0:T(8,128)(2,1)S(1)}, bf16[256,1024]{1,0:T(8,128)(2,1)S(1)}, u32[]{:S(2)}, u32[]{:S(2)}) collective-permute-start(bf16[256,1024]{1,0:T(8,128)(2,1)S(1)} %slice.57), channel_id=1, source_target_pairs={{0,1},{1,2},{2,3},{3,4},{4,5},{5,6},{6,7},{7,0},{8,9},{9,10},{10,1... | collective-permute-start | bytes 1572872 | tf_op jit(solution)/shard_map/ppermute | solution.py:200
  116.2 14.3 %collective-permute-start.31 = (bf16[256,1024]{1,0:T(8,128)(2,1)S(1)}, bf16[256,1024]{1,0:T(8,128)(2,1)S(1)}, u32[]{:S(2)}, u32[]{:S(2)}) collective-permute-start(bf16[256,1024]{1,0:T(8,128)(2,1)S(1)} %slice.58), channel_id=1, source_target_pairs={{0,7},{1,0},{2,1},{3,2},{4,3},{5,4},{6,5},{7,6},{8,15},{9,8},{10,9... | collective-permute-start | bytes 1572872 | tf_op jit(solution)/shard_map/ppermute | solution.py:204
  133.1 8.3 %collective-permute-start.32 = (bf16[64,1024]{1,0:T(8,128)(2,1)S(1)}, bf16[64,1024]{1,0:T(8,128)(2,1)S(1)}, u32[]{:S(2)}, u32[]{:S(2)}) collective-permute-start(bf16[64,1024]{1,0:T(8,128)(2,1)S(1)} %get-tuple-element.25), channel_id=1, source_target_pairs={{0,80},{8,248},{16,64},{24,232},{32,112},{40,216},{48,96},{56,200}... | collective-permute-start | bytes 393224 | tf_op jit(solution)/shard_map/ppermute | solution.py:50
  136.1 7.8 %collective-permute-start.33 = (bf16[64,1024]{1,0:T(8,128)(2,1)S(1)}, bf16[64,1024]{1,0:T(8,128)(2,1)S(1)}, u32[]{:S(2)}, u32[]{:S(2)}) collective-permute-start(bf16[64,1024]{1,0:T(8,128)(2,1)S(1)} %get-tuple-element.26), channel_id=1, source_target_pairs={{0,248},{8,80},{16,232},{24,64},{32,216},{40,112},{48,200},{56,96}... | collective-permute-start | bytes 393224 | tf_op jit(solution)/shard_map/ppermute | solution.py:50
  137.0 7.0 %collective-permute-start.34 = (bf16[64,1024]{1,0:T(8,128)(2,1)S(1)}, bf16[64,1024]{1,0:T(8,128)(2,1)S(1)}, u32[]{:S(2)}, u32[]{:S(2)}) collective-permute-start(bf16[64,1024]{1,0:T(8,128)(2,1)S(1)} %get-tuple-element.27), channel_id=1, source_target_pairs={{0,64},{8,200},{16,80},{24,216},{32,96},{40,232},{48,112},{56,248}... | collective-permute-start | bytes 393224 | tf_op jit(solution)/shard_map/ppermute | solution.py:50
  138.7 6.5 %collective-permute-start.35 = (bf16[64,1024]{1,0:T(8,128)(2,1)S(1)}, bf16[64,1024]{1,0:T(8,128)(2,1)S(1)}, u32[]{:S(2)}, u32[]{:S(2)}) collective-permute-start(bf16[64,1024]{1,0:T(8,128)(2,1)S(1)} %get-tuple-element.28), channel_id=1, source_target_pairs={{0,200},{8,64},{16,216},{24,80},{32,232},{40,96},{48,248},{56,112}... | collective-permute-start | bytes 393224 | tf_op jit(solution)/shard_map/ppermute | solution.py:50
  140.0 5.3 %collective-permute-start.36 = (bf16[64,1024]{1,0:T(8,128)(2,1)S(1)}, bf16[64,1024]{1,0:T(8,128)(2,1)S(1)}, u32[]{:S(2)}, u32[]{:S(2)}) collective-permute-start(bf16[64,1024]{1,0:T(8,128)(2,1)S(1)} %get-tuple-element.29), channel_id=1, source_target_pairs={{0,16},{8,56},{16,0},{24,40},{32,48},{40,24},{48,32},{56,8},{64,80... | collective-permute-start | bytes 393224 | tf_op jit(solution)/shard_map/ppermute | solution.py:50
  141.5 5.6 %collective-permute-start.37 = (bf16[64,1024]{1,0:T(8,128)(2,1)S(1)}, bf16[64,1024]{1,0:T(8,128)(2,1)S(1)}, u32[]{:S(2)}, u32[]{:S(2)}) collective-permute-start(bf16[64,1024]{1,0:T(8,128)(2,1)S(1)} %get-tuple-element.30), channel_id=1, source_target_pairs={{0,56},{8,16},{16,40},{24,0},{32,24},{40,48},{48,8},{56,32},{64,12... | collective-permute-start | bytes 393224 | tf_op jit(solution)/shard_map/ppermute | solution.py:50
  143.9 3.2 %collective-permute-start.38 = (bf16[64,1024]{1,0:T(8,128)(2,1)S(1)}, bf16[64,1024]{1,0:T(8,128)(2,1)S(1)}, u32[]{:S(2)}, u32[]{:S(2)}) collective-permute-start(bf16[64,1024]{1,0:T(8,128)(2,1)S(1)} %get-tuple-element.32), channel_id=1, source_target_pairs={{0,8},{8,0},{16,24},{24,16},{32,40},{40,32},{48,56},{56,48},{64,72... | collective-permute-start | bytes 393224 | tf_op jit(solution)/shard_map/ppermute | solution.py:50
  (12 other events, 19.5 us)
where the time goes:
time: 149 us
  starting transfers between devices  63.4 us (43%)
  waiting for transfers between devices  43.9 us (29%)
  Pallas kernels  19.9 us (13%)
  local copies, waits for them, and re-layouts  17.1 us (11%)
  other arithmetic  3.86 us (3%)
    ppermute x31, starting transfers between devices, send(): return lax.ppermute(a, 'seq', pairs)  42.3 us
    ppermute x31, waiting for transfers between devices, send(): return lax.ppermute(a, 'seq', pairs)  15.5 us
    ppermute x4, waiting for transfers between devices, up(): return lax.ppermute(a, 'tp', ring(lax.axis_size('tp'), 1))  14.2 us
    all_to_all x1, waiting for transfers between devices, per_device(): lax.all_to_all(attended, 'tp', split_axis=0, concat_axis=0, tiled=True)  14.1 us
    ppermute x4, starting transfers between devices, down(): return lax.ppermute(a, 'tp', ring(lax.axis_size('tp'), -1))  12.8 us
    pallas_call x2, Pallas kernels, project(): pl.pallas_call(functools.partial(project_kernel, steps, last), out_shape=...  10.3 us
    unnamed x41, local copies, waits for them, and re-layouts  9.68 us
    pallas_call x1, Pallas kernels, attend(): pl.pallas_call(attend_kernel, out_shape=jax.ShapeDtypeStruct((blocks, BLK...  9.6 us
  transfers between devices with their start and end apart: 40, of which 14 were waited for; matrix products, arithmetic and copies ran while one was open for 6% of the time, Pallas kernels for 12%

commit v1 on v0

--- a/solution.py
+++ b/solution.py
@@ -311,7 +311,6 @@
     w_u2, w_d2 = after([w_u2, w_d2], attended)
     w_u3, w_d3 = up(w_u2), down(w_d2)
     tokens = lax.all_to_all(attended, "tp", split_axis=0, concat_axis=0, tiled=True)
-    w_u3, w_d3 = after([w_u3, w_d3], tokens)
     w_u4, w_d4 = up(w_u3[:depth]), down(w_d3[depth:])
     group = [tokens] + [send(tokens, partner(r, 0)) for r in (1, 2, 3)]
     group += [send(a, SWAP) for a in group]

time: 149 us -> 145 us (0.973)
  local copies, waits for them, and re-layouts: 17.1 us -> 10.3 us
  waiting for transfers between devices: 43.9 us -> 48.3 us
  Pallas kernels: 19.9 us -> 17.3 us
    unnamed x41 -> x21, local copies, waits for them, and re-layouts: 9.68 us -> 4.04 us
    ppermute x4, waiting for transfers between devices: 14.2 us -> 17.8 us  [up(): return lax.ppermute(a, 'tp', ring(lax.axis_size('tp'), 1))]
    pallas_call x2, Pallas kernels: 10.3 us -> 7.68 us  [project(): pl.pallas_call(functools.partial(project_kernel, steps, last), out_shape=...]
  transfers between devices with their start and end apart: 40 -> 40, of which waited for: 14 -> 15; matrix products, arithmetic and copies ran while one was open for 6% -> 5% of each run, Pallas kernels for 12% -> 11%
where the time goes in v1:
time: 145 us; the launch traced here: 144 us
  starting transfers between devices  64.2 us (44%)
  waiting for transfers between devices  48.3 us (33%)
  Pallas kernels  17.3 us (12%)
  local copies, waits for them, and re-layouts  10.3 us (7%)
  other arithmetic  3.86 us (3%)
    ppermute x31, starting transfers between devices, send(): return lax.ppermute(a, 'seq', pairs)  42.6 us
    ppermute x4, waiting for transfers between devices, up(): return lax.ppermute(a, 'tp', ring(lax.axis_size('tp'), 1))  17.8 us
    ppermute x31, waiting for transfers between devices, send(): return lax.ppermute(a, 'seq', pairs)  15.2 us
    all_to_all x1, waiting for transfers between devices, per_device(): lax.all_to_all(attended, 'tp', split_axis=0, concat_axis=0, tiled=True)  14.9 us
    ppermute x4, starting transfers between devices, down(): return lax.ppermute(a, 'tp', ring(lax.axis_size('tp'), -1))  13.2 us
    pallas_call x1, Pallas kernels, attend(): pl.pallas_call(attend_kernel, out_shape=jax.ShapeDtypeStruct((blocks, BLK...  9.57 us
    pallas_call x2, Pallas kernels, project(): pl.pallas_call(functools.partial(project_kernel, steps, last), out_shape=...  7.68 us
    all_to_all x1, starting transfers between devices, per_device(): lax.all_to_all(attended, 'tp', split_axis=0, concat_axis=0, tiled=True)  6.49 us
  transfers between devices with their start and end apart: 40, of which 15 were waited for; matrix products, arithmetic and copies ran while one was open for 5% of the time, Pallas kernels for 11%

profile of v1, /device:TPU:1, one launch (start us, length us, event | category | flops | bytes accessed | tf_op | source)
XLA Modules:
  0.0 144.3 jit_solution(5218515875579432649)
XLA Ops:
  0.0 1.0 dynamic-slice_bitcast_fusion
  1.0 3.8 %collective-permute-start.2 = (bf16[2,512,128]{2,1,0:T(8,128)(2,1)S(1)}, bf16[2,512,128]{2,1,0:T(8,128)(2,1)S(1)}, u32[]{:S(2)}, u32[]{:S(2)}) collective-permute-start(bf16[2,512,128]{2,1,0:T(8,128)(2,1)S(1)} %dynamic-slice_bitcast_fusion), channel_id=1, source_target_pairs={{0,32},{8,136},{16,48},{24,152},{32,0},{40,168},{48,16},{56,184},{... | collective-permute-start | bytes 786440 | tf_op jit(solution)/shard_map/ppermute | solution.py:50
  4.8 0.8 collective-permute-start.1
  6.3 1.3 constant_dynamic-slice_fusion.refs_8_
  7.6 5.7 %collective-permute-start.25 = (bf16[512,1024]{1,0:T(8,128)(2,1)S(1)}, bf16[512,1024]{1,0:T(8,128)(2,1)}, u32[]{:S(2)}, u32[]{:S(2)}) collective-permute-start(bf16[512,1024]{1,0:T(8,128)(2,1)S(1)} %constant_dynamic-slice_fusion.refs_8_), channel_id=1, source_target_pairs={{0,7},{1,0},{2,1},{3,2},{4,3},{5,4},{6,5},{7,6},{8,15},{9,8},{10,9... | collective-permute-start | bytes 3145736 | tf_op jit(solution)/shard_map/ppermute | solution.py:204
  13.3 1.0 dynamic-slice_bitcast_fusion.1
  15.2 1.7 %collective-permute-start.9 = (bf16[4,512,128]{2,1,0:T(8,128)(2,1)S(1)}, bf16[4,512,128]{2,1,0:T(8,128)(2,1)}, u32[]{:S(2)}, u32[]{:S(2)}) collective-permute-start(bf16[4,512,128]{2,1,0:T(8,128)(2,1)S(1)} %pad_maximum_fusion.1.refs_0_), channel_id=1, source_target_pairs={{0,8},{8,0},{16,24},{24,16},{32,40},{40,32},{48,56},{56,48},{64,72... | collective-permute-start | bytes 1572872 | tf_op jit(solution)/shard_map/ppermute | solution.py:50
  16.9 2.1 %collective-permute-start.4 = (bf16[4,512,128]{2,1,0:T(8,128)(2,1)S(1)}, bf16[4,512,128]{2,1,0:T(8,128)(2,1)}, u32[]{:S(2)}, u32[]{:S(2)}) collective-permute-start(bf16[4,512,128]{2,1,0:T(8,128)(2,1)S(1)} %pad_maximum_fusion.1.refs_0_), channel_id=1, source_target_pairs={{0,192},{8,56},{16,208},{24,8},{32,224},{40,24},{48,240},{56,40},{... | collective-permute-start | bytes 1572872 | tf_op jit(solution)/shard_map/ppermute | solution.py:50
  19.3 1.0 pad_maximum_fusion.2.refs_4_
  20.3 1.1 collective-permute-start.13
  21.5 3.8 %collective-permute-done.4.refs_2_ = bf16[4,512,128]{2,1,0:T(8,128)(2,1)} collective-permute-done((bf16[4,512,128]{2,1,0:T(8,128)(2,1)S(1)}, bf16[4,512,128]{2,1,0:T(8,128)(2,1)}, u32[]{:S(2)}, u32[]{:S(2)}) %collective-permute-start.4) | collective-permute-done | bytes 524320 | tf_op jit(solution)/shard_map/ppermute | solution.py:50
  25.3 3.3 %collective-permute-start.7 = (bf16[4,512,128]{2,1,0:T(8,128)(2,1)S(1)}, bf16[4,512,128]{2,1,0:T(8,128)(2,1)}, u32[]{:S(2)}, u32[]{:S(2)}) collective-permute-start(bf16[4,512,128]{2,1,0:T(8,128)(2,1)S(1)} %pad_maximum_fusion.2.refs_4_), channel_id=1, source_target_pairs={{0,192},{8,56},{16,208},{24,8},{32,224},{40,24},{48,240},{56,40},{... | collective-permute-start | bytes 1572872 | tf_op jit(solution)/shard_map/ppermute | solution.py:50
  28.8 0.8 copy-done.4
  29.6 1.9 %collective-permute-start.11 = (bf16[4,512,128]{2,1,0:T(8,128)(2,1)}, bf16[4,512,128]{2,1,0:T(8,128)(2,1)}, u32[]{:S(2)}, u32[]{:S(2)}) collective-permute-start(bf16[4,512,128]{2,1,0:T(8,128)(2,1)} %collective-permute-done.4.refs_2_), channel_id=1, source_target_pairs={{0,8},{8,0},{16,24},{24,16},{32,40},{40,32},{48,56},{56,48},{64,72... | collective-permute-start | bytes 1572872 | tf_op jit(solution)/shard_map/ppermute | solution.py:50
  31.5 3.2 %collective-permute-done.7.refs_6_ = bf16[4,512,128]{2,1,0:T(8,128)(2,1)} collective-permute-done((bf16[4,512,128]{2,1,0:T(8,128)(2,1)S(1)}, bf16[4,512,128]{2,1,0:T(8,128)(2,1)}, u32[]{:S(2)}, u32[]{:S(2)}) %collective-permute-start.7) | collective-permute-done | bytes 524320 | tf_op jit(solution)/shard_map/ppermute | solution.py:50
  34.7 2.5 %collective-permute-start.10 = (bf16[4,512,128]{2,1,0:T(8,128)(2,1)S(1)}, bf16[4,512,128]{2,1,0:T(8,128)(2,1)}, u32[]{:S(2)}, u32[]{:S(2)}) collective-permute-start(bf16[4,512,128]{2,1,0:T(8,128)(2,1)S(1)} %collective-permute-done.3.refs_1_.refs_2_), channel_id=1, source_target_pairs={{0,8},{8,0},{16,24},{24,16},{32,40},{40,32},{48,56},{56,48},{64,72... | collective-permute-start | bytes 1572872 | tf_op jit(solution)/shard_map/ppermute | solution.py:50
  38.3 2.7 %collective-permute-start.15 = (bf16[4,512,128]{2,1,0:T(8,128)(2,1)}, bf16[4,512,128]{2,1,0:T(8,128)(2,1)}, u32[]{:S(2)}, u32[]{:S(2)}) collective-permute-start(bf16[4,512,128]{2,1,0:T(8,128)(2,1)} %collective-permute-done.7.refs_6_), channel_id=1, source_target_pairs={{0,8},{8,0},{16,24},{24,16},{32,40},{40,32},{48,56},{56,48},{64,72... | collective-permute-start | bytes 1572872 | tf_op jit(solution)/shard_map/ppermute | solution.py:50
  41.1 2.1 %collective-permute-start.8 = (bf16[4,512,128]{2,1,0:T(8,128)(2,1)}, bf16[4,512,128]{2,1,0:T(8,128)(2,1)}, u32[]{:S(2)}, u32[]{:S(2)}) collective-permute-start(bf16[4,512,128]{2,1,0:T(8,128)(2,1)} %collective-permute-done.7.refs_6_), channel_id=1, source_target_pairs={{0,192},{8,56},{16,208},{24,8},{32,224},{40,24},{48,240},{56,40},{... | collective-permute-start | bytes 1572872 | tf_op jit(solution)/shard_map/ppermute | solution.py:50
  43.7 3.3 %collective-permute-start.27 = (bf16[512,1024]{1,0:T(8,128)(2,1)}, bf16[512,1024]{1,0:T(8,128)(2,1)}, u32[]{:S(2)}, u32[]{:S(2)}) collective-permute-start(bf16[512,1024]{1,0:T(8,128)(2,1)} %get-tuple-element.18.refs_10_), channel_id=1, source_target_pairs={{0,7},{1,0},{2,1},{3,2},{4,3},{5,4},{6,5},{7,6},{8,15},{9,8},{10,9... | collective-permute-start | bytes 3145736 | tf_op jit(solution)/shard_map/ppermute | solution.py:204
  48.0 3.5 %collective-permute-start.14 = (bf16[4,512,128]{2,1,0:T(8,128)(2,1)}, bf16[4,512,128]{2,1,0:T(8,128)(2,1)S(1)}, u32[]{:S(2)}, u32[]{:S(2)}) collective-permute-start(bf16[4,512,128]{2,1,0:T(8,128)(2,1)} %copy-done.6), channel_id=1, source_target_pairs={{0,8},{8,0},{16,24},{24,16},{32,40},{40,32},{48,56},{56,48},{64,72... | collective-permute-start | bytes 1572872 | tf_op jit(solution)/shard_map/ppermute | solution.py:50
  52.1 1.1 collective-permute-done.14.refs_13_
  54.7 1.0 copy-done.2
  55.8 1.0 copy-done.5
  56.8 1.0 copy-done.7
  57.8 9.6 %attend.1.refs_2_ = bf16[8,64,512]{2,1,0:T(8,128)(2,1)} custom-call(s32[32]{0:T(128)S(1)} %fusion.4.slots_ref, s32[4,8]{1,0:T(4,128)S(1)} %copy.22.vert_ref, s32[32,8]{1,0:T(8,128)S(1)} %fusion.diag_ref, bf16[4,512,128]{2,1,0:T(8,128)(2,1)S(1)} %copy-done.3, s32[4,1,512]{2,1,0:T(1,128)S(1)} %add_select_fusion.1.kpv_ref, ...), custom_call_target="tpu_custom_call" | custom-call | flops 2147483648 | bytes 25165824 | tf_op jit(solution)/shard_map/attend/pallas_call | solution.py:161
  67.4 6.5 %all-to-all-start = ((bf16[8,64,512]{2,1,0:T(8,128)(2,1)}), bf16[8,64,512]{2,1,0:T(8,128)(2,1)S(1)}, u32[]{:S(2)}, u32[]{:S(2)}) async-start(bf16[8,64,512]{2,1,0:T(8,128)(2,1)} %attend.1.refs_2_), calls=%async_computation | async-start | bytes 1048576 | tf_op jit(solution)/shard_map/all_to_all | solution.py:313
  73.9 1.5 %collective-permute-start.28 = (bf16[512,1024]{1,0:T(8,128)(2,1)}, bf16[512,1024]{1,0:T(8,128)(2,1)S(1)}, u32[]{:S(2)}, u32[]{:S(2)}) collective-permute-start(bf16[512,1024]{1,0:T(8,128)(2,1)} %get-tuple-element.19.refs_11_), channel_id=1, source_target_pairs={{0,1},{1,2},{2,3},{3,4},{4,5},{5,6},{6,7},{7,0},{8,9},{9,10},{10,1... | collective-permute-start | bytes 3145736 | tf_op jit(solution)/shard_map/ppermute | solution.py:200
  75.5 1.3 collective-permute-start.30
  76.8 14.9 %all-to-all-done.refs_0_ = bf16[8,64,512]{2,1,0:T(8,128)(2,1)S(1)} async-done(((bf16[8,64,512]{2,1,0:T(8,128)(2,1)}), bf16[8,64,512]{2,1,0:T(8,128)(2,1)S(1)}, u32[]{:S(2)}, u32[]{:S(2)}) %all-to-all-start) | async-done | bytes 524320 | tf_op jit(solution)/shard_map/all_to_all | solution.py:313
  91.7 2.9 %collective-permute-start.19 = (bf16[8,64,512]{2,1,0:T(8,128)(2,1)S(1)}, bf16[8,64,512]{2,1,0:T(8,128)(2,1)S(1)}, u32[]{:S(2)}, u32[]{:S(2)}) collective-permute-start(bf16[8,64,512]{2,1,0:T(8,128)(2,1)S(1)} %all-to-all-done.refs_0_), channel_id=1, source_target_pairs={{0,80},{8,248},{16,64},{24,232},{32,112},{40,216},{48,96},{56,200}... | collective-permute-start | bytes 1572872 | tf_op jit(solution)/shard_map/ppermute | solution.py:50
  94.6 0.9 collective-permute-start.18
  95.5 1.3 collective-permute-start.17
  96.8 14.0 %collective-permute-done.28.refs_13_ = bf16[512,1024]{1,0:T(8,128)(2,1)S(1)} collective-permute-done((bf16[512,1024]{1,0:T(8,128)(2,1)}, bf16[512,1024]{1,0:T(8,128)(2,1)S(1)}, u32[]{:S(2)}, u32[]{:S(2)}) %collective-permute-start.28) | collective-permute-done | bytes 1048608 | tf_op jit(solution)/shard_map/ppermute | solution.py:200
  110.7 1.4 collective-permute-start.20
  112.9 1.1 slice.76
  114.0 3.0 %collective-permute-start.31 = (bf16[256,1024]{1,0:T(8,128)(2,1)S(1)}, bf16[256,1024]{1,0:T(8,128)(2,1)S(1)}, u32[]{:S(2)}, u32[]{:S(2)}) collective-permute-start(bf16[256,1024]{1,0:T(8,128)(2,1)S(1)} %slice.76), channel_id=1, source_target_pairs={{0,7},{1,0},{2,1},{3,2},{4,3},{5,4},{6,5},{7,6},{8,15},{9,8},{10,9... | collective-permute-start | bytes 1572872 | tf_op jit(solution)/shard_map/ppermute | solution.py:204
  117.0 6.3 %project.2.refs_10_ = f32[512,1024]{1,0:T(8,128)S(1)} custom-call(s32[2]{0:T(128)S(1)} %pad_add_fusion.place_ref, bf16[8,64,512]{2,1,0:T(8,128)(2,1)S(1)} %all-to-all-done.refs_0_, bf16[8,64,512]{2,1,0:T(8,128)(2,1)S(1)} %collective-permute-done.17.refs_1_, bf16[8,64,512]{2,1,0:T(8,128)(2,1)S(1)} %collective-permute-done.18.refs_2_, ...), custom_call_target="tpu_custom_call" | custom-call | flops 3758096384 | bytes 14680064 | tf_op jit(solution)/shard_map/project/pallas_call | solution.py:260
  123.3 3.8 %collective-permute-done.29.refs_8_ = bf16[256,1024]{1,0:T(8,128)(2,1)S(1)} collective-permute-done((bf16[256,1024]{1,0:T(8,128)(2,1)S(1)}, bf16[256,1024]{1,0:T(8,128)(2,1)S(1)}, u32[]{:S(2)}, u32[]{:S(2)}) %collective-permute-start.29) | collective-permute-done | bytes 524320 | tf_op jit(solution)/shard_map/ppermute | solution.py:200
  127.5 1.4 project.3
  128.9 3.0 %collective-permute-start.32 = (bf16[64,1024]{1,0:T(8,128)(2,1)S(1)}, bf16[64,1024]{1,0:T(8,128)(2,1)S(1)}, u32[]{:S(2)}, u32[]{:S(2)}) collective-permute-start(bf16[64,1024]{1,0:T(8,128)(2,1)S(1)} %get-tuple-element.21), channel_id=1, source_target_pairs={{0,80},{8,248},{16,64},{24,232},{32,112},{40,216},{48,96},{56,200}... | collective-permute-start | bytes 393224 | tf_op jit(solution)/shard_map/ppermute | solution.py:50
  131.9 1.2 collective-permute-start.33
  133.1 1.8 %collective-permute-start.34 = (bf16[64,1024]{1,0:T(8,128)(2,1)S(1)}, bf16[64,1024]{1,0:T(8,128)(2,1)S(1)}, u32[]{:S(2)}, u32[]{:S(2)}) collective-permute-start(bf16[64,1024]{1,0:T(8,128)(2,1)S(1)} %get-tuple-element.23), channel_id=1, source_target_pairs={{0,64},{8,200},{16,80},{24,216},{32,96},{40,232},{48,112},{56,248}... | collective-permute-start | bytes 393224 | tf_op jit(solution)/shard_map/ppermute | solution.py:50
  134.8 0.9 collective-permute-start.35
  135.8 1.4 %collective-permute-start.36 = (bf16[64,1024]{1,0:T(8,128)(2,1)S(1)}, bf16[64,1024]{1,0:T(8,128)(2,1)S(1)}, u32[]{:S(2)}, u32[]{:S(2)}) collective-permute-start(bf16[64,1024]{1,0:T(8,128)(2,1)S(1)} %get-tuple-element.25), channel_id=1, source_target_pairs={{0,16},{8,56},{16,0},{24,40},{32,48},{40,24},{48,32},{56,8},{64,80... | collective-permute-start | bytes 393224 | tf_op jit(solution)/shard_map/ppermute | solution.py:50
  137.8 1.9 %collective-permute-done.33 = bf16[64,1024]{1,0:T(8,128)(2,1)S(1)} collective-permute-done((bf16[64,1024]{1,0:T(8,128)(2,1)S(1)}, bf16[64,1024]{1,0:T(8,128)(2,1)S(1)}, u32[]{:S(2)}, u32[]{:S(2)}) %collective-permute-start.33) | collective-permute-done | bytes 131104 | tf_op jit(solution)/shard_map/ppermute | solution.py:50
  139.7 1.3 collective-permute-done.35
  141.0 1.8 %collective-permute-done.37 = bf16[64,1024]{1,0:T(8,128)(2,1)S(1)} collective-permute-done((bf16[64,1024]{1,0:T(8,128)(2,1)S(1)}, bf16[64,1024]{1,0:T(8,128)(2,1)S(1)}, u32[]{:S(2)}, u32[]{:S(2)}) %collective-permute-start.37) | collective-permute-done | bytes 131104 | tf_op jit(solution)/shard_map/ppermute | solution.py:50
  143.3 1.0 pad_maximum_fusion
  (103 shorter events, 9.1 us)
Async XLA Ops:
  0.0 14.3 %copy-start = (s32[32,8]{0,1:T(8,128)S(1)}, s32[32,8]{0,1:T(8,128)}, u32[]{:S(2)}) copy-start(s32[32,8]{0,1:T(8,128)} %param.9) | copy-start | bytes 3076
  1.0 13.4 %collective-permute-start.2 = (bf16[2,512,128]{2,1,0:T(8,128)(2,1)S(1)}, bf16[2,512,128]{2,1,0:T(8,128)(2,1)S(1)}, u32[]{:S(2)}, u32[]{:S(2)}) collective-permute-start(bf16[2,512,128]{2,1,0:T(8,128)(2,1)S(1)} %dynamic-slice_bitcast_fusion), channel_id=1, source_target_pairs={{0,32},{8,136},{16,48},{24,152},{32,0},{40,168},{48,16},{56,184},{... | collective-permute-start | bytes 786440 | tf_op jit(solution)/shard_map/ppermute | solution.py:50
  4.8 9.5 %collective-permute-start.1 = (bf16[2,512,128]{2,1,0:T(8,128)(2,1)S(1)}, bf16[2,512,128]{2,1,0:T(8,128)(2,1)S(1)}, u32[]{:S(2)}, u32[]{:S(2)}) collective-permute-start(bf16[2,512,128]{2,1,0:T(8,128)(2,1)S(1)} %dynamic-slice_bitcast_fusion), channel_id=1, source_target_pairs={{0,48},{8,200},{16,0},{24,216},{32,16},{40,232},{48,32},{56,248},{... | collective-permute-start | bytes 786440 | tf_op jit(solution)/shard_map/ppermute | solution.py:50
  5.6 8.8 %collective-permute-start = (bf16[2,512,128]{2,1,0:T(8,128)(2,1)S(1)}, bf16[2,512,128]{2,1,0:T(8,128)(2,1)S(1)}, u32[]{:S(2)}, u32[]{:S(2)}) collective-permute-start(bf16[2,512,128]{2,1,0:T(8,128)(2,1)S(1)} %dynamic-slice_bitcast_fusion), channel_id=1, source_target_pairs={{0,16},{8,72},{16,32},{24,88},{32,48},{40,104},{48,0},{56,120},{64... | collective-permute-start | bytes 786440 | tf_op jit(solution)/shard_map/ppermute | solution.py:50
  7.6 11.4 %copy-start.8 = (s32[32,8]{0,1:T(8,128)S(1)}, s32[32,8]{0,1:T(8,128)}, u32[]{:S(2)}) copy-start(s32[32,8]{0,1:T(8,128)} %param.10) | copy-start | bytes 3076
  7.6 11.5 %copy-start.9 = (s32[32,2]{0,1:T(2,128)S(1)}, s32[32,2]{0,1:T(2,128)}, u32[]{:S(2)}) copy-start(s32[32,2]{0,1:T(2,128)} %param.11) | copy-start | bytes 772
  7.6 30.7 %collective-permute-start.25 = (bf16[512,1024]{1,0:T(8,128)(2,1)S(1)}, bf16[512,1024]{1,0:T(8,128)(2,1)}, u32[]{:S(2)}, u32[]{:S(2)}) collective-permute-start(bf16[512,1024]{1,0:T(8,128)(2,1)S(1)} %constant_dynamic-slice_fusion.refs_8_), channel_id=1, source_target_pairs={{0,7},{1,0},{2,1},{3,2},{4,3},{5,4},{6,5},{7,6},{8,15},{9,8},{10,9... | collective-permute-start | bytes 3145736 | tf_op jit(solution)/shard_map/ppermute | solution.py:204
  13.3 27.8 %collective-permute-start.24 = (bf16[512,1024]{1,0:T(8,128)(2,1)S(1)}, bf16[512,1024]{1,0:T(8,128)(2,1)}, u32[]{:S(2)}, u32[]{:S(2)}) collective-permute-start(bf16[512,1024]{1,0:T(8,128)(2,1)S(1)} %constant_dynamic-slice_fusion.refs_8_), channel_id=1, source_target_pairs={{0,1},{1,2},{2,3},{3,4},{4,5},{5,6},{6,7},{7,0},{8,9},{9,10},{10,1... | collective-permute-start | bytes 3145736 | tf_op jit(solution)/shard_map/ppermute | solution.py:200
  15.2 5.2 %collective-permute-start.9 = (bf16[4,512,128]{2,1,0:T(8,128)(2,1)S(1)}, bf16[4,512,128]{2,1,0:T(8,128)(2,1)}, u32[]{:S(2)}, u32[]{:S(2)}) collective-permute-start(bf16[4,512,128]{2,1,0:T(8,128)(2,1)S(1)} %pad_maximum_fusion.1.refs_0_), channel_id=1, source_target_pairs={{0,8},{8,0},{16,24},{24,16},{32,40},{40,32},{48,56},{56,48},{64,72... | collective-permute-start | bytes 1572872 | tf_op jit(solution)/shard_map/ppermute | solution.py:50
  16.9 8.4 %collective-permute-start.4 = (bf16[4,512,128]{2,1,0:T(8,128)(2,1)S(1)}, bf16[4,512,128]{2,1,0:T(8,128)(2,1)}, u32[]{:S(2)}, u32[]{:S(2)}) collective-permute-start(bf16[4,512,128]{2,1,0:T(8,128)(2,1)S(1)} %pad_maximum_fusion.1.refs_0_), channel_id=1, source_target_pairs={{0,192},{8,56},{16,208},{24,8},{32,224},{40,24},{48,240},{56,40},{... | collective-permute-start | bytes 1572872 | tf_op jit(solution)/shard_map/ppermute | solution.py:50
  19.0 9.7 %collective-permute-start.3 = (bf16[4,512,128]{2,1,0:T(8,128)(2,1)S(1)}, bf16[4,512,128]{2,1,0:T(8,128)(2,1)S(1)}, u32[]{:S(2)}, u32[]{:S(2)}) collective-permute-start(bf16[4,512,128]{2,1,0:T(8,128)(2,1)S(1)} %pad_maximum_fusion.1.refs_0_), channel_id=1, source_target_pairs={{0,64},{8,24},{16,80},{24,40},{32,96},{40,56},{48,112},{56,8},{64,... | collective-permute-start | bytes 1572872 | tf_op jit(solution)/shard_map/ppermute | solution.py:50
  19.3 35.4 %copy-start.3 = (bf16[4,512,128]{2,1,0:T(8,128)(2,1)S(1)}, bf16[4,512,128]{2,1,0:T(8,128)(2,1)}, u32[]{:S(2)}) copy-start(bf16[4,512,128]{2,1,0:T(8,128)(2,1)} %q_ref.1) | copy-start | bytes 1572868
  20.3 8.5 %collective-permute-start.13 = (bf16[4,512,128]{2,1,0:T(8,128)(2,1)S(1)}, bf16[4,512,128]{2,1,0:T(8,128)(2,1)S(1)}, u32[]{:S(2)}, u32[]{:S(2)}) collective-permute-start(bf16[4,512,128]{2,1,0:T(8,128)(2,1)S(1)} %pad_maximum_fusion.2.refs_4_), channel_id=1, source_target_pairs={{0,8},{8,0},{16,24},{24,16},{32,40},{40,32},{48,56},{56,48},{64,72... | collective-permute-start | bytes 1572872 | tf_op jit(solution)/shard_map/ppermute | solution.py:50
  25.3 9.4 %collective-permute-start.7 = (bf16[4,512,128]{2,1,0:T(8,128)(2,1)S(1)}, bf16[4,512,128]{2,1,0:T(8,128)(2,1)}, u32[]{:S(2)}, u32[]{:S(2)}) collective-permute-start(bf16[4,512,128]{2,1,0:T(8,128)(2,1)S(1)} %pad_maximum_fusion.2.refs_4_), channel_id=1, source_target_pairs={{0,192},{8,56},{16,208},{24,8},{32,224},{40,24},{48,240},{56,40},{... | collective-permute-start | bytes 1572872 | tf_op jit(solution)/shard_map/ppermute | solution.py:50
  28.7 14.7 %copy-start.1 = (bf16[4,512,128]{2,1,0:T(8,128)(2,1)}, bf16[4,512,128]{2,1,0:T(8,128)(2,1)S(1)}, u32[]{:S(2)}) copy-start(bf16[4,512,128]{2,1,0:T(8,128)(2,1)S(1)} %collective-permute-done.3.refs_1_.refs_2_) | copy-start | bytes 1572868
  28.7 9.6 %collective-permute-start.6 = (bf16[4,512,128]{2,1,0:T(8,128)(2,1)S(1)}, bf16[4,512,128]{2,1,0:T(8,128)(2,1)S(1)}, u32[]{:S(2)}, u32[]{:S(2)}) collective-permute-start(bf16[4,512,128]{2,1,0:T(8,128)(2,1)S(1)} %pad_maximum_fusion.2.refs_4_), channel_id=1, source_target_pairs={{0,64},{8,24},{16,80},{24,40},{32,96},{40,56},{48,112},{56,8},{64,... | collective-permute-start | bytes 1572872 | tf_op jit(solution)/shard_map/ppermute | solution.py:50
  29.6 13.7 %collective-permute-start.11 = (bf16[4,512,128]{2,1,0:T(8,128)(2,1)}, bf16[4,512,128]{2,1,0:T(8,128)(2,1)}, u32[]{:S(2)}, u32[]{:S(2)}) collective-permute-start(bf16[4,512,128]{2,1,0:T(8,128)(2,1)} %collective-permute-done.4.refs_2_), channel_id=1, source_target_pairs={{0,8},{8,0},{16,24},{24,16},{32,40},{40,32},{48,56},{56,48},{64,72... | collective-permute-start | bytes 1572872 | tf_op jit(solution)/shard_map/ppermute | solution.py:50
  34.7 8.9 %collective-permute-start.10 = (bf16[4,512,128]{2,1,0:T(8,128)(2,1)S(1)}, bf16[4,512,128]{2,1,0:T(8,128)(2,1)}, u32[]{:S(2)}, u32[]{:S(2)}) collective-permute-start(bf16[4,512,128]{2,1,0:T(8,128)(2,1)S(1)} %collective-permute-done.3.refs_1_.refs_2_), channel_id=1, source_target_pairs={{0,8},{8,0},{16,24},{24,16},{32,40},{40,32},{48,56},{56,48},{64,72... | collective-permute-start | bytes 1572872 | tf_op jit(solution)/shard_map/ppermute | solution.py:50
  38.3 2.7 %copy-start.6 = (bf16[4,512,128]{2,1,0:T(8,128)(2,1)}, bf16[4,512,128]{2,1,0:T(8,128)(2,1)S(1)}, u32[]{:S(2)}) copy-start(bf16[4,512,128]{2,1,0:T(8,128)(2,1)S(1)} %collective-permute-done.6.refs_5_) | copy-start | bytes 1572868
  38.3 9.6 %collective-permute-start.5 = (bf16[4,512,128]{2,1,0:T(8,128)(2,1)S(1)}, bf16[4,512,128]{2,1,0:T(8,128)(2,1)}, u32[]{:S(2)}, u32[]{:S(2)}) collective-permute-start(bf16[4,512,128]{2,1,0:T(8,128)(2,1)S(1)} %collective-permute-done.3.refs_1_.refs_2_), channel_id=1, source_target_pairs={{0,64},{8,24},{16,80},{24,40},{32,96},{40,56},{48,112},{56,8},{64,... | collective-permute-start | bytes 1572872 | tf_op jit(solution)/shard_map/ppermute | solution.py:50
  38.3 13.1 %collective-permute-start.15 = (bf16[4,512,128]{2,1,0:T(8,128)(2,1)}, bf16[4,512,128]{2,1,0:T(8,128)(2,1)}, u32[]{:S(2)}, u32[]{:S(2)}) collective-permute-start(bf16[4,512,128]{2,1,0:T(8,128)(2,1)} %collective-permute-done.7.refs_6_), channel_id=1, source_target_pairs={{0,8},{8,0},{16,24},{24,16},{32,40},{40,32},{48,56},{56,48},{64,72... | collective-permute-start | bytes 1572872 | tf_op jit(solution)/shard_map/ppermute | solution.py:50
  41.1 10.4 %collective-permute-start.8 = (bf16[4,512,128]{2,1,0:T(8,128)(2,1)}, bf16[4,512,128]{2,1,0:T(8,128)(2,1)}, u32[]{:S(2)}, u32[]{:S(2)}) collective-permute-start(bf16[4,512,128]{2,1,0:T(8,128)(2,1)} %collective-permute-done.7.refs_6_), channel_id=1, source_target_pairs={{0,192},{8,56},{16,208},{24,8},{32,224},{40,24},{48,240},{56,40},{... | collective-permute-start | bytes 1572872 | tf_op jit(solution)/shard_map/ppermute | solution.py:50
  43.4 30.5 %collective-permute-start.26 = (bf16[512,1024]{1,0:T(8,128)(2,1)}, bf16[512,1024]{1,0:T(8,128)(2,1)}, u32[]{:S(2)}, u32[]{:S(2)}) collective-permute-start(bf16[512,1024]{1,0:T(8,128)(2,1)} %get-tuple-element.17.refs_9_), channel_id=1, source_target_pairs={{0,1},{1,2},{2,3},{3,4},{4,5},{5,6},{6,7},{7,0},{8,9},{9,10},{10,1... | collective-permute-start | bytes 3145736 | tf_op jit(solution)/shard_map/ppermute | solution.py:200
  43.7 30.3 %collective-permute-start.27 = (bf16[512,1024]{1,0:T(8,128)(2,1)}, bf16[512,1024]{1,0:T(8,128)(2,1)}, u32[]{:S(2)}, u32[]{:S(2)}) collective-permute-start(bf16[512,1024]{1,0:T(8,128)(2,1)} %get-tuple-element.18.refs_10_), channel_id=1, source_target_pairs={{0,7},{1,0},{2,1},{3,2},{4,3},{5,4},{6,5},{7,6},{8,15},{9,8},{10,9... | collective-permute-start | bytes 3145736 | tf_op jit(solution)/shard_map/ppermute | solution.py:204
  48.0 5.2 %collective-permute-start.14 = (bf16[4,512,128]{2,1,0:T(8,128)(2,1)}, bf16[4,512,128]{2,1,0:T(8,128)(2,1)S(1)}, u32[]{:S(2)}, u32[]{:S(2)}) collective-permute-start(bf16[4,512,128]{2,1,0:T(8,128)(2,1)} %copy-done.6), channel_id=1, source_target_pairs={{0,8},{8,0},{16,24},{24,16},{32,40},{40,32},{48,56},{56,48},{64,72... | collective-permute-start | bytes 1572872 | tf_op jit(solution)/shard_map/ppermute | solution.py:50
  51.5 2.5 %collective-permute-start.12 = (bf16[4,512,128]{2,1,0:T(8,128)(2,1)}, bf16[4,512,128]{2,1,0:T(8,128)(2,1)S(1)}, u32[]{:S(2)}, u32[]{:S(2)}) collective-permute-start(bf16[4,512,128]{2,1,0:T(8,128)(2,1)} %collective-permute-done.5.refs_3_), channel_id=1, source_target_pairs={{0,8},{8,0},{16,24},{24,16},{32,40},{40,32},{48,56},{56,48},{64,72... | collective-permute-start | bytes 1572872 | tf_op jit(solution)/shard_map/ppermute | solution.py:50
  51.5 3.2 %collective-permute-start.16 = (bf16[4,512,128]{2,1,0:T(8,128)(2,1)}, bf16[4,512,128]{2,1,0:T(8,128)(2,1)S(1)}, u32[]{:S(2)}, u32[]{:S(2)}) collective-permute-start(bf16[4,512,128]{2,1,0:T(8,128)(2,1)} %collective-permute-done.8.refs_7_), channel_id=1, source_target_pairs={{0,8},{8,0},{16,24},{24,16},{32,40},{40,32},{48,56},{56,48},{64,72... | collective-permute-start | bytes 1572872 | tf_op jit(solution)/shard_map/ppermute | solution.py:50
  54.7 1.0 copy-start.2
  55.7 1.0 copy-start.5
  67.4 24.3 %all-to-all-start = ((bf16[8,64,512]{2,1,0:T(8,128)(2,1)}), bf16[8,64,512]{2,1,0:T(8,128)(2,1)S(1)}, u32[]{:S(2)}, u32[]{:S(2)}) async-start(bf16[8,64,512]{2,1,0:T(8,128)(2,1)} %attend.1.refs_2_), calls=%async_computation | async-start | bytes 1048576 | tf_op jit(solution)/shard_map/all_to_all | solution.py:313
  73.9 36.8 %collective-permute-start.28 = (bf16[512,1024]{1,0:T(8,128)(2,1)}, bf16[512,1024]{1,0:T(8,128)(2,1)S(1)}, u32[]{:S(2)}, u32[]{:S(2)}) collective-permute-start(bf16[512,1024]{1,0:T(8,128)(2,1)} %get-tuple-element.19.refs_11_), channel_id=1, source_target_pairs={{0,1},{1,2},{2,3},{3,4},{4,5},{5,6},{6,7},{7,0},{8,9},{9,10},{10,1... | collective-permute-start | bytes 3145736 | tf_op jit(solution)/shard_map/ppermute | solution.py:200
  75.5 37.3 %collective-permute-start.30 = (bf16[512,1024]{1,0:T(8,128)(2,1)}, bf16[512,1024]{1,0:T(8,128)(2,1)}, u32[]{:S(2)}, u32[]{:S(2)}) collective-permute-start(bf16[512,1024]{1,0:T(8,128)(2,1)} %get-tuple-element.20.refs_12_), channel_id=1, source_target_pairs={{0,7},{1,0},{2,1},{3,2},{4,3},{5,4},{6,5},{7,6},{8,15},{9,8},{10,9... | collective-permute-start | bytes 3145736 | tf_op jit(solution)/shard_map/ppermute | solution.py:204
  91.7 20.4 %collective-permute-start.19 = (bf16[8,64,512]{2,1,0:T(8,128)(2,1)S(1)}, bf16[8,64,512]{2,1,0:T(8,128)(2,1)S(1)}, u32[]{:S(2)}, u32[]{:S(2)}) collective-permute-start(bf16[8,64,512]{2,1,0:T(8,128)(2,1)S(1)} %all-to-all-done.refs_0_), channel_id=1, source_target_pairs={{0,80},{8,248},{16,64},{24,232},{32,112},{40,216},{48,96},{56,200}... | collective-permute-start | bytes 1572872 | tf_op jit(solution)/shard_map/ppermute | solution.py:50
  94.6 17.5 %collective-permute-start.18 = (bf16[8,64,512]{2,1,0:T(8,128)(2,1)S(1)}, bf16[8,64,512]{2,1,0:T(8,128)(2,1)S(1)}, u32[]{:S(2)}, u32[]{:S(2)}) collective-permute-start(bf16[8,64,512]{2,1,0:T(8,128)(2,1)S(1)} %all-to-all-done.refs_0_), channel_id=1, source_target_pairs={{0,64},{8,200},{16,80},{24,216},{32,96},{40,232},{48,112},{56,248}... | collective-permute-start | bytes 1572872 | tf_op jit(solution)/shard_map/ppermute | solution.py:50
  95.5 17.1 %collective-permute-start.17 = (bf16[8,64,512]{2,1,0:T(8,128)(2,1)S(1)}, bf16[8,64,512]{2,1,0:T(8,128)(2,1)S(1)}, u32[]{:S(2)}, u32[]{:S(2)}) collective-permute-start(bf16[8,64,512]{2,1,0:T(8,128)(2,1)S(1)} %all-to-all-done.refs_0_), channel_id=1, source_target_pairs={{0,16},{8,56},{16,0},{24,40},{32,48},{40,24},{48,32},{56,8},{64,80... | collective-permute-start | bytes 1572872 | tf_op jit(solution)/shard_map/ppermute | solution.py:50
  110.7 3.2 %collective-permute-start.20 = (bf16[8,64,512]{2,1,0:T(8,128)(2,1)S(1)}, bf16[8,64,512]{2,1,0:T(8,128)(2,1)S(1)}, u32[]{:S(2)}, u32[]{:S(2)}) collective-permute-start(bf16[8,64,512]{2,1,0:T(8,128)(2,1)S(1)} %all-to-all-done.refs_0_), channel_id=1, source_target_pairs={{0,8},{8,0},{16,24},{24,16},{32,40},{40,32},{48,56},{56,48},{64,72... | collective-permute-start | bytes 1572872 | tf_op jit(solution)/shard_map/ppermute | solution.py:50
  112.1 4.9 %collective-permute-start.23 = (bf16[8,64,512]{2,1,0:T(8,128)(2,1)S(1)}, bf16[8,64,512]{2,1,0:T(8,128)(2,1)S(1)}, u32[]{:S(2)}, u32[]{:S(2)}) collective-permute-start(bf16[8,64,512]{2,1,0:T(8,128)(2,1)S(1)} %collective-permute-done.19.refs_3_), channel_id=1, source_target_pairs={{0,8},{8,0},{16,24},{24,16},{32,40},{40,32},{48,56},{56,48},{64,72... | collective-permute-start | bytes 1572872 | tf_op jit(solution)/shard_map/ppermute | solution.py:50
  112.1 4.9 %collective-permute-start.22 = (bf16[8,64,512]{2,1,0:T(8,128)(2,1)S(1)}, bf16[8,64,512]{2,1,0:T(8,128)(2,1)S(1)}, u32[]{:S(2)}, u32[]{:S(2)}) collective-permute-start(bf16[8,64,512]{2,1,0:T(8,128)(2,1)S(1)} %collective-permute-done.18.refs_2_), channel_id=1, source_target_pairs={{0,8},{8,0},{16,24},{24,16},{32,40},{40,32},{48,56},{56,48},{64,72... | collective-permute-start | bytes 1572872 | tf_op jit(solution)/shard_map/ppermute | solution.py:50
  112.7 4.4 %collective-permute-start.21 = (bf16[8,64,512]{2,1,0:T(8,128)(2,1)S(1)}, bf16[8,64,512]{2,1,0:T(8,128)(2,1)S(1)}, u32[]{:S(2)}, u32[]{:S(2)}) collective-permute-start(bf16[8,64,512]{2,1,0:T(8,128)(2,1)S(1)} %collective-permute-done.17.refs_1_), channel_id=1, source_target_pairs={{0,8},{8,0},{16,24},{24,16},{32,40},{40,32},{48,56},{56,48},{64,72... | collective-permute-start | bytes 1572872 | tf_op jit(solution)/shard_map/ppermute | solution.py:50
  112.8 14.4 %collective-permute-start.29 = (bf16[256,1024]{1,0:T(8,128)(2,1)S(1)}, bf16[256,1024]{1,0:T(8,128)(2,1)S(1)}, u32[]{:S(2)}, u32[]{:S(2)}) collective-permute-start(bf16[256,1024]{1,0:T(8,128)(2,1)S(1)} %slice.75), channel_id=1, source_target_pairs={{0,1},{1,2},{2,3},{3,4},{4,5},{5,6},{6,7},{7,0},{8,9},{9,10},{10,1... | collective-permute-start | bytes 1572872 | tf_op jit(solution)/shard_map/ppermute | solution.py:200
  114.0 13.5 %collective-permute-start.31 = (bf16[256,1024]{1,0:T(8,128)(2,1)S(1)}, bf16[256,1024]{1,0:T(8,128)(2,1)S(1)}, u32[]{:S(2)}, u32[]{:S(2)}) collective-permute-start(bf16[256,1024]{1,0:T(8,128)(2,1)S(1)} %slice.76), channel_id=1, source_target_pairs={{0,7},{1,0},{2,1},{3,2},{4,3},{5,4},{6,5},{7,6},{8,15},{9,8},{10,9... | collective-permute-start | bytes 1572872 | tf_op jit(solution)/shard_map/ppermute | solution.py:204
  128.9 8.3 %collective-permute-start.32 = (bf16[64,1024]{1,0:T(8,128)(2,1)S(1)}, bf16[64,1024]{1,0:T(8,128)(2,1)S(1)}, u32[]{:S(2)}, u32[]{:S(2)}) collective-permute-start(bf16[64,1024]{1,0:T(8,128)(2,1)S(1)} %get-tuple-element.21), channel_id=1, source_target_pairs={{0,80},{8,248},{16,64},{24,232},{32,112},{40,216},{48,96},{56,200}... | collective-permute-start | bytes 393224 | tf_op jit(solution)/shard_map/ppermute | solution.py:50
  131.9 7.8 %collective-permute-start.33 = (bf16[64,1024]{1,0:T(8,128)(2,1)S(1)}, bf16[64,1024]{1,0:T(8,128)(2,1)S(1)}, u32[]{:S(2)}, u32[]{:S(2)}) collective-permute-start(bf16[64,1024]{1,0:T(8,128)(2,1)S(1)} %get-tuple-element.22), channel_id=1, source_target_pairs={{0,248},{8,80},{16,232},{24,64},{32,216},{40,112},{48,200},{56,96}... | collective-permute-start | bytes 393224 | tf_op jit(solution)/shard_map/ppermute | solution.py:50
  133.1 6.6 %collective-permute-start.34 = (bf16[64,1024]{1,0:T(8,128)(2,1)S(1)}, bf16[64,1024]{1,0:T(8,128)(2,1)S(1)}, u32[]{:S(2)}, u32[]{:S(2)}) collective-permute-start(bf16[64,1024]{1,0:T(8,128)(2,1)S(1)} %get-tuple-element.23), channel_id=1, source_target_pairs={{0,64},{8,200},{16,80},{24,216},{32,96},{40,232},{48,112},{56,248}... | collective-permute-start | bytes 393224 | tf_op jit(solution)/shard_map/ppermute | solution.py:50
  134.8 6.2 %collective-permute-start.35 = (bf16[64,1024]{1,0:T(8,128)(2,1)S(1)}, bf16[64,1024]{1,0:T(8,128)(2,1)S(1)}, u32[]{:S(2)}, u32[]{:S(2)}) collective-permute-start(bf16[64,1024]{1,0:T(8,128)(2,1)S(1)} %get-tuple-element.24), channel_id=1, source_target_pairs={{0,200},{8,64},{16,216},{24,80},{32,232},{40,96},{48,248},{56,112}... | collective-permute-start | bytes 393224 | tf_op jit(solution)/shard_map/ppermute | solution.py:50
  135.8 5.3 %collective-permute-start.36 = (bf16[64,1024]{1,0:T(8,128)(2,1)S(1)}, bf16[64,1024]{1,0:T(8,128)(2,1)S(1)}, u32[]{:S(2)}, u32[]{:S(2)}) collective-permute-start(bf16[64,1024]{1,0:T(8,128)(2,1)S(1)} %get-tuple-element.25), channel_id=1, source_target_pairs={{0,16},{8,56},{16,0},{24,40},{32,48},{40,24},{48,32},{56,8},{64,80... | collective-permute-start | bytes 393224 | tf_op jit(solution)/shard_map/ppermute | solution.py:50
  137.2 5.6 %collective-permute-start.37 = (bf16[64,1024]{1,0:T(8,128)(2,1)S(1)}, bf16[64,1024]{1,0:T(8,128)(2,1)S(1)}, u32[]{:S(2)}, u32[]{:S(2)}) collective-permute-start(bf16[64,1024]{1,0:T(8,128)(2,1)S(1)} %get-tuple-element.26), channel_id=1, source_target_pairs={{0,56},{8,16},{16,40},{24,0},{32,24},{40,48},{48,8},{56,32},{64,12... | collective-permute-start | bytes 393224 | tf_op jit(solution)/shard_map/ppermute | solution.py:50
  139.7 3.2 %collective-permute-start.38 = (bf16[64,1024]{1,0:T(8,128)(2,1)S(1)}, bf16[64,1024]{1,0:T(8,128)(2,1)S(1)}, u32[]{:S(2)}, u32[]{:S(2)}) collective-permute-start(bf16[64,1024]{1,0:T(8,128)(2,1)S(1)} %get-tuple-element.28), channel_id=1, source_target_pairs={{0,8},{8,0},{16,24},{24,16},{32,40},{40,32},{48,56},{56,48},{64,72... | collective-permute-start | bytes 393224 | tf_op jit(solution)/shard_map/ppermute | solution.py:50
  (2 other events, 1.9 us)

commit v2 on v1

--- a/solution.py
+++ b/solution.py
@@ -298,7 +298,6 @@
     far_k, far_v = send(up_k, B_UP), send(down_v, B_DOWN)
     pieces = [line_k, up_k, down_k, far_k, line_v, up_v, down_v, far_v]
     pieces += [send(a, SWAP) for a in pieces]
-    w_u1, w_d1 = after([w_u1, w_d1], up_k)
     w_u2, w_d2 = up(w_u1), down(w_d1)
 
     def mine(a):

time: 145 us -> 146 us (level)
  starting transfers between devices: 64.2 us -> 56.7 us
  waiting for transfers between devices: 48.3 us -> 55.7 us
  local copies, waits for them, and re-layouts: 10.3 us -> 13.7 us
    ppermute x31, waiting for transfers between devices: 15.2 us -> 23.1 us  [send(): return lax.ppermute(a, 'seq', pairs)]
    ppermute x31, starting transfers between devices: 42.6 us -> 35.8 us  [send(): return lax.ppermute(a, 'seq', pairs)]
    unnamed x21 -> x29, local copies, waits for them, and re-layouts: 4.04 us -> 6.98 us
    ppermute x4, starting transfers between devices: 13.2 us -> 11.6 us  [down(): return lax.ppermute(a, 'tp', ring(lax.axis_size('tp'), -1))]
  transfers between devices with their start and end apart: 40 -> 40, of which waited for: 15 -> 16; matrix products, arithmetic and copies ran while one was open for 5% -> 5% of each run, Pallas kernels for 11% -> 10%
where the time goes in v2:
time: 146 us
  starting transfers between devices  56.7 us (39%)
  waiting for transfers between devices  55.7 us (38%)
  Pallas kernels  16.6 us (11%)
  local copies, waits for them, and re-layouts  13.7 us (9%)
  other arithmetic  2.9 us (2%)
    ppermute x31, starting transfers between devices, send(): return lax.ppermute(a, 'seq', pairs)  35.8 us
    ppermute x31, waiting for transfers between devices, send(): return lax.ppermute(a, 'seq', pairs)  23.1 us
    ppermute x4, waiting for transfers between devices, up(): return lax.ppermute(a, 'tp', ring(lax.axis_size('tp'), 1))  18.2 us
    all_to_all x1, waiting for transfers between devices, per_device(): lax.all_to_all(attended, 'tp', split_axis=0, concat_axis=0, tiled=True)  14.1 us
    ppermute x4, starting transfers between devices, down(): return lax.ppermute(a, 'tp', ring(lax.axis_size('tp'), -1))  11.6 us
    pallas_call x1, Pallas kernels, attend(): pl.pallas_call(attend_kernel, out_shape=jax.ShapeDtypeStruct((blocks, BLK...  9.25 us
    pallas_call x2, Pallas kernels, project(): pl.pallas_call(functools.partial(project_kernel, steps, last), out_shape=...  7.32 us
    unnamed x29, local copies, waits for them, and re-layouts  6.98 us
  transfers between devices with their start and end apart: 40, of which 16 were waited for; matrix products, arithmetic and copies ran while one was open for 5% of the time, Pallas kernels for 10%

profile of v2, /device:TPU:1, one launch (start us, length us, event | category | flops | bytes accessed | tf_op | source)
XLA Modules:
  0.0 145.9 jit_solution(12509290832937474888)
XLA Ops:
  0.0 1.0 dynamic-slice_bitcast_fusion
  1.0 2.2 %collective-permute-start = (bf16[2,512,128]{2,1,0:T(8,128)(2,1)S(1)}, bf16[2,512,128]{2,1,0:T(8,128)(2,1)S(1)}, u32[]{:S(2)}, u32[]{:S(2)}) collective-permute-start(bf16[2,512,128]{2,1,0:T(8,128)(2,1)S(1)} %dynamic-slice_bitcast_fusion), channel_id=1, source_target_pairs={{0,16},{8,72},{16,32},{24,88},{32,48},{40,104},{48,0},{56,120},{64... | collective-permute-start | bytes 786440 | tf_op jit(solution)/shard_map/ppermute | solution.py:50
  3.2 1.5 %collective-permute-start.1 = (bf16[2,512,128]{2,1,0:T(8,128)(2,1)S(1)}, bf16[2,512,128]{2,1,0:T(8,128)(2,1)S(1)}, u32[]{:S(2)}, u32[]{:S(2)}) collective-permute-start(bf16[2,512,128]{2,1,0:T(8,128)(2,1)S(1)} %dynamic-slice_bitcast_fusion), channel_id=1, source_target_pairs={{0,48},{8,200},{16,0},{24,216},{32,16},{40,232},{48,32},{56,248},{... | collective-permute-start | bytes 786440 | tf_op jit(solution)/shard_map/ppermute | solution.py:50
  4.7 1.6 %collective-permute-start.2 = (bf16[2,512,128]{2,1,0:T(8,128)(2,1)S(1)}, bf16[2,512,128]{2,1,0:T(8,128)(2,1)S(1)}, u32[]{:S(2)}, u32[]{:S(2)}) collective-permute-start(bf16[2,512,128]{2,1,0:T(8,128)(2,1)S(1)} %dynamic-slice_bitcast_fusion), channel_id=1, source_target_pairs={{0,32},{8,136},{16,48},{24,152},{32,0},{40,168},{48,16},{56,184},{... | collective-permute-start | bytes 786440 | tf_op jit(solution)/shard_map/ppermute | solution.py:50
  6.3 1.3 constant_dynamic-slice_fusion.refs_8_
  7.6 1.7 %collective-permute-start.24 = (bf16[512,1024]{1,0:T(8,128)(2,1)S(1)}, bf16[512,1024]{1,0:T(8,128)(2,1)S(1)}, u32[]{:S(2)}, u32[]{:S(2)}) collective-permute-start(bf16[512,1024]{1,0:T(8,128)(2,1)S(1)} %constant_dynamic-slice_fusion.refs_8_), channel_id=1, source_target_pairs={{0,1},{1,2},{2,3},{3,4},{4,5},{5,6},{6,7},{7,0},{8,9},{9,10},{10,1... | collective-permute-start | bytes 3145736 | tf_op jit(solution)/shard_map/ppermute | solution.py:200
  9.3 4.0 %collective-permute-start.26 = (bf16[512,1024]{1,0:T(8,128)(2,1)S(1)}, bf16[512,1024]{1,0:T(8,128)(2,1)}, u32[]{:S(2)}, u32[]{:S(2)}) collective-permute-start(bf16[512,1024]{1,0:T(8,128)(2,1)S(1)} %constant_dynamic-slice_fusion.refs_8_), channel_id=1, source_target_pairs={{0,7},{1,0},{2,1},{3,2},{4,3},{5,4},{6,5},{7,6},{8,15},{9,8},{10,9... | collective-permute-start | bytes 3145736 | tf_op jit(solution)/shard_map/ppermute | solution.py:204
  13.3 1.0 dynamic-slice_bitcast_fusion.1
  14.6 2.6 %collective-permute-start.7 = (bf16[4,512,128]{2,1,0:T(8,128)(2,1)S(1)}, bf16[4,512,128]{2,1,0:T(8,128)(2,1)}, u32[]{:S(2)}, u32[]{:S(2)}) collective-permute-start(bf16[4,512,128]{2,1,0:T(8,128)(2,1)S(1)} %pad_maximum_fusion.2.refs_4_), channel_id=1, source_target_pairs={{0,192},{8,56},{16,208},{24,8},{32,224},{40,24},{48,240},{56,40},{... | collective-permute-start | bytes 1572872 | tf_op jit(solution)/shard_map/ppermute | solution.py:50
  17.8 5.5 %collective-permute-done.7.refs_6_ = bf16[4,512,128]{2,1,0:T(8,128)(2,1)} collective-permute-done((bf16[4,512,128]{2,1,0:T(8,128)(2,1)S(1)}, bf16[4,512,128]{2,1,0:T(8,128)(2,1)}, u32[]{:S(2)}, u32[]{:S(2)}) %collective-permute-start.7) | collective-permute-done | bytes 524320 | tf_op jit(solution)/shard_map/ppermute | solution.py:50
  23.3 2.7 %collective-permute-start.13 = (bf16[4,512,128]{2,1,0:T(8,128)(2,1)S(1)}, bf16[4,512,128]{2,1,0:T(8,128)(2,1)S(1)}, u32[]{:S(2)}, u32[]{:S(2)}) collective-permute-start(bf16[4,512,128]{2,1,0:T(8,128)(2,1)S(1)} %pad_maximum_fusion.2.refs_4_), channel_id=1, source_target_pairs={{0,8},{8,0},{16,24},{24,16},{32,40},{40,32},{48,56},{56,48},{64,72... | collective-permute-start | bytes 1572872 | tf_op jit(solution)/shard_map/ppermute | solution.py:50
  27.2 5.3 %collective-permute-done.3.refs_1_ = bf16[4,512,128]{2,1,0:T(8,128)(2,1)} collective-permute-done((bf16[4,512,128]{2,1,0:T(8,128)(2,1)S(1)}, bf16[4,512,128]{2,1,0:T(8,128)(2,1)}, u32[]{:S(2)}, u32[]{:S(2)}) %collective-permute-start.3) | collective-permute-done | bytes 524320 | tf_op jit(solution)/shard_map/ppermute | solution.py:50
  32.4 3.0 %collective-permute-start.9 = (bf16[4,512,128]{2,1,0:T(8,128)(2,1)S(1)}, bf16[4,512,128]{2,1,0:T(8,128)(2,1)S(1)}, u32[]{:S(2)}, u32[]{:S(2)}) collective-permute-start(bf16[4,512,128]{2,1,0:T(8,128)(2,1)S(1)} %pad_maximum_fusion.1.refs_0_), channel_id=1, source_target_pairs={{0,8},{8,0},{16,24},{24,16},{32,40},{40,32},{48,56},{56,48},{64,72... | collective-permute-start | bytes 1572872 | tf_op jit(solution)/shard_map/ppermute | solution.py:50
  37.2 1.8 %collective-permute-start.14 = (bf16[4,512,128]{2,1,0:T(8,128)(2,1)}, bf16[4,512,128]{2,1,0:T(8,128)(2,1)}, u32[]{:S(2)}, u32[]{:S(2)}) collective-permute-start(bf16[4,512,128]{2,1,0:T(8,128)(2,1)} %collective-permute-done.6.refs_5_), channel_id=1, source_target_pairs={{0,8},{8,0},{16,24},{24,16},{32,40},{40,32},{48,56},{56,48},{64,72... | collective-permute-start | bytes 1572872 | tf_op jit(solution)/shard_map/ppermute | solution.py:50
  41.5 3.5 %collective-permute-done.8.refs_7_ = bf16[4,512,128]{2,1,0:T(8,128)(2,1)} collective-permute-done((bf16[4,512,128]{2,1,0:T(8,128)(2,1)}, bf16[4,512,128]{2,1,0:T(8,128)(2,1)}, u32[]{:S(2)}, u32[]{:S(2)}) %collective-permute-start.8) | collective-permute-done | bytes 524320 | tf_op jit(solution)/shard_map/ppermute | solution.py:50
  45.0 3.4 %collective-permute-start.27 = (bf16[512,1024]{1,0:T(8,128)(2,1)}, bf16[512,1024]{1,0:T(8,128)(2,1)}, u32[]{:S(2)}, u32[]{:S(2)}) collective-permute-start(bf16[512,1024]{1,0:T(8,128)(2,1)} %collective-permute-done.26.refs_10_), channel_id=1, source_target_pairs={{0,7},{1,0},{2,1},{3,2},{4,3},{5,4},{6,5},{7,6},{8,15},{9,8},{10,9... | collective-permute-start | bytes 3145736 | tf_op jit(solution)/shard_map/ppermute | solution.py:204
  49.3 1.2 collective-permute-start.11
  50.5 1.2 collective-permute-start.16
  52.3 1.2 collective-permute-done.16.refs_15_
  54.3 1.0 copy-done.3
  55.3 1.0 copy-done.5
  56.4 1.0 copy-done.7
  57.4 1.0 copy-done.9
  58.4 9.2 %attend.1.refs_2_ = bf16[8,64,512]{2,1,0:T(8,128)(2,1)} custom-call(s32[32]{0:T(128)S(1)} %fusion.4.slots_ref, s32[4,8]{1,0:T(4,128)S(1)} %copy.20.vert_ref, s32[32,8]{1,0:T(8,128)S(1)} %fusion.diag_ref, bf16[4,512,128]{2,1,0:T(8,128)(2,1)S(1)} %copy-done.3, s32[4,1,512]{2,1,0:T(1,128)S(1)} %add_select_fusion.1.kpv_ref, ...), custom_call_target="tpu_custom_call" | custom-call | flops 2147483648 | bytes 25165824 | tf_op jit(solution)/shard_map/attend/pallas_call | solution.py:161
  67.7 6.0 %all-to-all-start = ((bf16[8,64,512]{2,1,0:T(8,128)(2,1)}), bf16[8,64,512]{2,1,0:T(8,128)(2,1)S(1)}, u32[]{:S(2)}, u32[]{:S(2)}) async-start(bf16[8,64,512]{2,1,0:T(8,128)(2,1)} %attend.1.refs_2_), calls=%async_computation | async-start | bytes 1048576 | tf_op jit(solution)/shard_map/all_to_all | solution.py:312
  74.7 1.5 collective-permute-start.28
  76.2 1.2 collective-permute-start.30
  77.4 14.1 %all-to-all-done.refs_0_ = bf16[8,64,512]{2,1,0:T(8,128)(2,1)S(1)} async-done(((bf16[8,64,512]{2,1,0:T(8,128)(2,1)}), bf16[8,64,512]{2,1,0:T(8,128)(2,1)S(1)}, u32[]{:S(2)}, u32[]{:S(2)}) %all-to-all-start) | async-done | bytes 524320 | tf_op jit(solution)/shard_map/all_to_all | solution.py:312
  91.5 2.0 %collective-permute-start.17 = (bf16[8,64,512]{2,1,0:T(8,128)(2,1)S(1)}, bf16[8,64,512]{2,1,0:T(8,128)(2,1)S(1)}, u32[]{:S(2)}, u32[]{:S(2)}) collective-permute-start(bf16[8,64,512]{2,1,0:T(8,128)(2,1)S(1)} %all-to-all-done.refs_0_), channel_id=1, source_target_pairs={{0,16},{8,56},{16,0},{24,40},{32,48},{40,24},{48,32},{56,8},{64,80... | collective-permute-start | bytes 1572872 | tf_op jit(solution)/shard_map/ppermute | solution.py:50
  93.5 3.1 %collective-permute-start.19 = (bf16[8,64,512]{2,1,0:T(8,128)(2,1)S(1)}, bf16[8,64,512]{2,1,0:T(8,128)(2,1)S(1)}, u32[]{:S(2)}, u32[]{:S(2)}) collective-permute-start(bf16[8,64,512]{2,1,0:T(8,128)(2,1)S(1)} %all-to-all-done.refs_0_), channel_id=1, source_target_pairs={{0,80},{8,248},{16,64},{24,232},{32,112},{40,216},{48,96},{56,200}... | collective-permute-start | bytes 1572872 | tf_op jit(solution)/shard_map/ppermute | solution.py:50
  96.6 14.1 %collective-permute-done.28.refs_13_ = bf16[512,1024]{1,0:T(8,128)(2,1)} collective-permute-done((bf16[512,1024]{1,0:T(8,128)(2,1)}, bf16[512,1024]{1,0:T(8,128)(2,1)}, u32[]{:S(2)}, u32[]{:S(2)}) %collective-permute-start.28) | collective-permute-done | bytes 1048608 | tf_op jit(solution)/shard_map/ppermute | solution.py:200
  110.6 1.4 collective-permute-start.20
  112.7 1.1 slice.75
  113.8 1.1 slice.76
  114.9 3.0 %collective-permute-start.31 = (bf16[256,1024]{1,0:T(8,128)(2,1)S(1)}, bf16[256,1024]{1,0:T(8,128)(2,1)S(1)}, u32[]{:S(2)}, u32[]{:S(2)}) collective-permute-start(bf16[256,1024]{1,0:T(8,128)(2,1)S(1)} %slice.76), channel_id=1, source_target_pairs={{0,7},{1,0},{2,1},{3,2},{4,3},{5,4},{6,5},{7,6},{8,15},{9,8},{10,9... | collective-permute-start | bytes 1572872 | tf_op jit(solution)/shard_map/ppermute | solution.py:204
  118.0 6.0 %project.2.refs_10_ = f32[512,1024]{1,0:T(8,128)S(1)} custom-call(s32[2]{0:T(128)S(1)} %pad_add_fusion.place_ref, bf16[8,64,512]{2,1,0:T(8,128)(2,1)S(1)} %all-to-all-done.refs_0_, bf16[8,64,512]{2,1,0:T(8,128)(2,1)S(1)} %collective-permute-done.17.refs_1_, bf16[8,64,512]{2,1,0:T(8,128)(2,1)S(1)} %collective-permute-done.18.refs_2_, ...), custom_call_target="tpu_custom_call" | custom-call | flops 3758096384 | bytes 14680064 | tf_op jit(solution)/shard_map/project/pallas_call | solution.py:260
  124.0 4.2 %collective-permute-done.29.refs_8_ = bf16[256,1024]{1,0:T(8,128)(2,1)S(1)} collective-permute-done((bf16[256,1024]{1,0:T(8,128)(2,1)S(1)}, bf16[256,1024]{1,0:T(8,128)(2,1)S(1)}, u32[]{:S(2)}, u32[]{:S(2)}) %collective-permute-start.29) | collective-permute-done | bytes 524320 | tf_op jit(solution)/shard_map/ppermute | solution.py:200
  128.4 1.4 project.3
  129.8 2.1 %collective-permute-start.36 = (bf16[64,1024]{1,0:T(8,128)(2,1)S(1)}, bf16[64,1024]{1,0:T(8,128)(2,1)S(1)}, u32[]{:S(2)}, u32[]{:S(2)}) collective-permute-start(bf16[64,1024]{1,0:T(8,128)(2,1)S(1)} %get-tuple-element.21), channel_id=1, source_target_pairs={{0,16},{8,56},{16,0},{24,40},{32,48},{40,24},{48,32},{56,8},{64,80... | collective-permute-start | bytes 393224 | tf_op jit(solution)/shard_map/ppermute | solution.py:50
  131.9 1.2 collective-permute-start.37
  133.1 1.7 %collective-permute-start.32 = (bf16[64,1024]{1,0:T(8,128)(2,1)S(1)}, bf16[64,1024]{1,0:T(8,128)(2,1)S(1)}, u32[]{:S(2)}, u32[]{:S(2)}) collective-permute-start(bf16[64,1024]{1,0:T(8,128)(2,1)S(1)} %get-tuple-element.17), channel_id=1, source_target_pairs={{0,80},{8,248},{16,64},{24,232},{32,112},{40,216},{48,96},{56,200}... | collective-permute-start | bytes 393224 | tf_op jit(solution)/shard_map/ppermute | solution.py:50
  134.8 1.3 collective-permute-start.33
  136.2 1.4 collective-permute-start.34
  137.5 1.3 collective-permute-done.37
  138.8 1.1 collective-permute-start.35
  140.3 2.3 %collective-permute-done.33 = bf16[64,1024]{1,0:T(8,128)(2,1)S(1)} collective-permute-done((bf16[64,1024]{1,0:T(8,128)(2,1)S(1)}, bf16[64,1024]{1,0:T(8,128)(2,1)S(1)}, u32[]{:S(2)}, u32[]{:S(2)}) %collective-permute-start.33) | collective-permute-done | bytes 131104 | tf_op jit(solution)/shard_map/ppermute | solution.py:50
  143.1 1.4 collective-permute-done.35
  144.9 1.0 pad_maximum_fusion
  (110 shorter events, 11.7 us)
Async XLA Ops:
  0.0 14.3 %copy-start = (s32[32,8]{0,1:T(8,128)S(1)}, s32[32,8]{0,1:T(8,128)}, u32[]{:S(2)}) copy-start(s32[32,8]{0,1:T(8,128)} %param.10) | copy-start | bytes 3076
  1.0 13.4 %collective-permute-start = (bf16[2,512,128]{2,1,0:T(8,128)(2,1)S(1)}, bf16[2,512,128]{2,1,0:T(8,128)(2,1)S(1)}, u32[]{:S(2)}, u32[]{:S(2)}) collective-permute-start(bf16[2,512,128]{2,1,0:T(8,128)(2,1)S(1)} %dynamic-slice_bitcast_fusion), channel_id=1, source_target_pairs={{0,16},{8,72},{16,32},{24,88},{32,48},{40,104},{48,0},{56,120},{64... | collective-permute-start | bytes 786440 | tf_op jit(solution)/shard_map/ppermute | solution.py:50
  3.2 11.3 %collective-permute-start.1 = (bf16[2,512,128]{2,1,0:T(8,128)(2,1)S(1)}, bf16[2,512,128]{2,1,0:T(8,128)(2,1)S(1)}, u32[]{:S(2)}, u32[]{:S(2)}) collective-permute-start(bf16[2,512,128]{2,1,0:T(8,128)(2,1)S(1)} %dynamic-slice_bitcast_fusion), channel_id=1, source_target_pairs={{0,48},{8,200},{16,0},{24,216},{32,16},{40,232},{48,32},{56,248},{... | collective-permute-start | bytes 786440 | tf_op jit(solution)/shard_map/ppermute | solution.py:50
  4.7 9.8 %collective-permute-start.2 = (bf16[2,512,128]{2,1,0:T(8,128)(2,1)S(1)}, bf16[2,512,128]{2,1,0:T(8,128)(2,1)S(1)}, u32[]{:S(2)}, u32[]{:S(2)}) collective-permute-start(bf16[2,512,128]{2,1,0:T(8,128)(2,1)S(1)} %dynamic-slice_bitcast_fusion), channel_id=1, source_target_pairs={{0,32},{8,136},{16,48},{24,152},{32,0},{40,168},{48,16},{56,184},{... | collective-permute-start | bytes 786440 | tf_op jit(solution)/shard_map/ppermute | solution.py:50
  7.6 33.0 %collective-permute-start.24 = (bf16[512,1024]{1,0:T(8,128)(2,1)S(1)}, bf16[512,1024]{1,0:T(8,128)(2,1)S(1)}, u32[]{:S(2)}, u32[]{:S(2)}) collective-permute-start(bf16[512,1024]{1,0:T(8,128)(2,1)S(1)} %constant_dynamic-slice_fusion.refs_8_), channel_id=1, source_target_pairs={{0,1},{1,2},{2,3},{3,4},{4,5},{5,6},{6,7},{7,0},{8,9},{9,10},{10,1... | collective-permute-start | bytes 3145736 | tf_op jit(solution)/shard_map/ppermute | solution.py:200
  9.3 31.7 %collective-permute-start.26 = (bf16[512,1024]{1,0:T(8,128)(2,1)S(1)}, bf16[512,1024]{1,0:T(8,128)(2,1)}, u32[]{:S(2)}, u32[]{:S(2)}) collective-permute-start(bf16[512,1024]{1,0:T(8,128)(2,1)S(1)} %constant_dynamic-slice_fusion.refs_8_), channel_id=1, source_target_pairs={{0,7},{1,0},{2,1},{3,2},{4,3},{5,4},{6,5},{7,6},{8,15},{9,8},{10,9... | collective-permute-start | bytes 3145736 | tf_op jit(solution)/shard_map/ppermute | solution.py:204
  13.3 4.2 %copy-start.12 = (s32[32,8]{0,1:T(8,128)S(1)}, s32[32,8]{0,1:T(8,128)}, u32[]{:S(2)}) copy-start(s32[32,8]{0,1:T(8,128)} %param.9) | copy-start | bytes 3076
  13.3 4.4 %copy-start.13 = (s32[32,2]{0,1:T(2,128)S(1)}, s32[32,2]{0,1:T(2,128)}, u32[]{:S(2)}) copy-start(s32[32,2]{0,1:T(2,128)} %param.11) | copy-start | bytes 772
  14.6 8.7 %collective-permute-start.7 = (bf16[4,512,128]{2,1,0:T(8,128)(2,1)S(1)}, bf16[4,512,128]{2,1,0:T(8,128)(2,1)}, u32[]{:S(2)}, u32[]{:S(2)}) collective-permute-start(bf16[4,512,128]{2,1,0:T(8,128)(2,1)S(1)} %pad_maximum_fusion.2.refs_4_), channel_id=1, source_target_pairs={{0,192},{8,56},{16,208},{24,8},{32,224},{40,24},{48,240},{56,40},{... | collective-permute-start | bytes 1572872 | tf_op jit(solution)/shard_map/ppermute | solution.py:50
  17.2 9.6 %collective-permute-start.6 = (bf16[4,512,128]{2,1,0:T(8,128)(2,1)S(1)}, bf16[4,512,128]{2,1,0:T(8,128)(2,1)}, u32[]{:S(2)}, u32[]{:S(2)}) collective-permute-start(bf16[4,512,128]{2,1,0:T(8,128)(2,1)S(1)} %pad_maximum_fusion.2.refs_4_), channel_id=1, source_target_pairs={{0,64},{8,24},{16,80},{24,40},{32,96},{40,56},{48,112},{56,8},{64,... | collective-permute-start | bytes 1572872 | tf_op jit(solution)/shard_map/ppermute | solution.py:50
  17.2 15.2 %collective-permute-start.3 = (bf16[4,512,128]{2,1,0:T(8,128)(2,1)S(1)}, bf16[4,512,128]{2,1,0:T(8,128)(2,1)}, u32[]{:S(2)}, u32[]{:S(2)}) collective-permute-start(bf16[4,512,128]{2,1,0:T(8,128)(2,1)S(1)} %pad_maximum_fusion.1.refs_0_), channel_id=1, source_target_pairs={{0,64},{8,24},{16,80},{24,40},{32,96},{40,56},{48,112},{56,8},{64,... | collective-permute-start | bytes 1572872 | tf_op jit(solution)/shard_map/ppermute | solution.py:50
  23.3 12.3 %collective-permute-start.13 = (bf16[4,512,128]{2,1,0:T(8,128)(2,1)S(1)}, bf16[4,512,128]{2,1,0:T(8,128)(2,1)S(1)}, u32[]{:S(2)}, u32[]{:S(2)}) collective-permute-start(bf16[4,512,128]{2,1,0:T(8,128)(2,1)S(1)} %pad_maximum_fusion.2.refs_4_), channel_id=1, source_target_pairs={{0,8},{8,0},{16,24},{24,16},{32,40},{40,32},{48,56},{56,48},{64,72... | collective-permute-start | bytes 1572872 | tf_op jit(solution)/shard_map/ppermute | solution.py:50
  26.8 10.4 %collective-permute-start.4 = (bf16[4,512,128]{2,1,0:T(8,128)(2,1)S(1)}, bf16[4,512,128]{2,1,0:T(8,128)(2,1)S(1)}, u32[]{:S(2)}, u32[]{:S(2)}) collective-permute-start(bf16[4,512,128]{2,1,0:T(8,128)(2,1)S(1)} %pad_maximum_fusion.1.refs_0_), channel_id=1, source_target_pairs={{0,192},{8,56},{16,208},{24,8},{32,224},{40,24},{48,240},{56,40},{... | collective-permute-start | bytes 1572872 | tf_op jit(solution)/shard_map/ppermute | solution.py:50
  32.4 7.3 %collective-permute-start.9 = (bf16[4,512,128]{2,1,0:T(8,128)(2,1)S(1)}, bf16[4,512,128]{2,1,0:T(8,128)(2,1)S(1)}, u32[]{:S(2)}, u32[]{:S(2)}) collective-permute-start(bf16[4,512,128]{2,1,0:T(8,128)(2,1)S(1)} %pad_maximum_fusion.1.refs_0_), channel_id=1, source_target_pairs={{0,8},{8,0},{16,24},{24,16},{32,40},{40,32},{48,56},{56,48},{64,72... | collective-permute-start | bytes 1572872 | tf_op jit(solution)/shard_map/ppermute | solution.py:50
  36.4 8.6 %collective-permute-start.8 = (bf16[4,512,128]{2,1,0:T(8,128)(2,1)}, bf16[4,512,128]{2,1,0:T(8,128)(2,1)}, u32[]{:S(2)}, u32[]{:S(2)}) collective-permute-start(bf16[4,512,128]{2,1,0:T(8,128)(2,1)} %collective-permute-done.7.refs_6_), channel_id=1, source_target_pairs={{0,192},{8,56},{16,208},{24,8},{32,224},{40,24},{48,240},{56,40},{... | collective-permute-start | bytes 1572872 | tf_op jit(solution)/shard_map/ppermute | solution.py:50
  37.2 3.7 %copy-start.6 = (bf16[4,512,128]{2,1,0:T(8,128)(2,1)}, bf16[4,512,128]{2,1,0:T(8,128)(2,1)S(1)}, u32[]{:S(2)}) copy-start(bf16[4,512,128]{2,1,0:T(8,128)(2,1)S(1)} %collective-permute-done.4.refs_2_) | copy-start | bytes 1572868
  37.2 7.8 %collective-permute-start.14 = (bf16[4,512,128]{2,1,0:T(8,128)(2,1)}, bf16[4,512,128]{2,1,0:T(8,128)(2,1)}, u32[]{:S(2)}, u32[]{:S(2)}) collective-permute-start(bf16[4,512,128]{2,1,0:T(8,128)(2,1)} %collective-permute-done.6.refs_5_), channel_id=1, source_target_pairs={{0,8},{8,0},{16,24},{24,16},{32,40},{40,32},{48,56},{56,48},{64,72... | collective-permute-start | bytes 1572872 | tf_op jit(solution)/shard_map/ppermute | solution.py:50
  40.5 8.8 %collective-permute-start.15 = (bf16[4,512,128]{2,1,0:T(8,128)(2,1)}, bf16[4,512,128]{2,1,0:T(8,128)(2,1)}, u32[]{:S(2)}, u32[]{:S(2)}) collective-permute-start(bf16[4,512,128]{2,1,0:T(8,128)(2,1)} %collective-permute-done.7.refs_6_), channel_id=1, source_target_pairs={{0,8},{8,0},{16,24},{24,16},{32,40},{40,32},{48,56},{56,48},{64,72... | collective-permute-start | bytes 1572872 | tf_op jit(solution)/shard_map/ppermute | solution.py:50
  40.6 10.0 %collective-permute-start.5 = (bf16[4,512,128]{2,1,0:T(8,128)(2,1)}, bf16[4,512,128]{2,1,0:T(8,128)(2,1)}, u32[]{:S(2)}, u32[]{:S(2)}) collective-permute-start(bf16[4,512,128]{2,1,0:T(8,128)(2,1)} %collective-permute-done.3.refs_1_), channel_id=1, source_target_pairs={{0,64},{8,24},{16,80},{24,40},{32,96},{40,56},{48,112},{56,8},{64,... | collective-permute-start | bytes 1572872 | tf_op jit(solution)/shard_map/ppermute | solution.py:50
  41.0 10.8 %collective-permute-start.10 = (bf16[4,512,128]{2,1,0:T(8,128)(2,1)}, bf16[4,512,128]{2,1,0:T(8,128)(2,1)}, u32[]{:S(2)}, u32[]{:S(2)}) collective-permute-start(bf16[4,512,128]{2,1,0:T(8,128)(2,1)} %collective-permute-done.3.refs_1_), channel_id=1, source_target_pairs={{0,8},{8,0},{16,24},{24,16},{32,40},{40,32},{48,56},{56,48},{64,72... | collective-permute-start | bytes 1572872 | tf_op jit(solution)/shard_map/ppermute | solution.py:50
  45.0 28.7 %collective-permute-start.25 = (bf16[512,1024]{1,0:T(8,128)(2,1)}, bf16[512,1024]{1,0:T(8,128)(2,1)S(1)}, u32[]{:S(2)}, u32[]{:S(2)}) collective-permute-start(bf16[512,1024]{1,0:T(8,128)(2,1)} %copy-done.10), channel_id=1, source_target_pairs={{0,1},{1,2},{2,3},{3,4},{4,5},{5,6},{6,7},{7,0},{8,9},{9,10},{10,1... | collective-permute-start | bytes 3145736 | tf_op jit(solution)/shard_map/ppermute | solution.py:200
  45.0 28.7 %collective-permute-start.27 = (bf16[512,1024]{1,0:T(8,128)(2,1)}, bf16[512,1024]{1,0:T(8,128)(2,1)}, u32[]{:S(2)}, u32[]{:S(2)}) collective-permute-start(bf16[512,1024]{1,0:T(8,128)(2,1)} %collective-permute-done.26.refs_10_), channel_id=1, source_target_pairs={{0,7},{1,0},{2,1},{3,2},{4,3},{5,4},{6,5},{7,6},{8,15},{9,8},{10,9... | collective-permute-start | bytes 3145736 | tf_op jit(solution)/shard_map/ppermute | solution.py:204
  49.3 3.0 %collective-permute-start.11 = (bf16[4,512,128]{2,1,0:T(8,128)(2,1)}, bf16[4,512,128]{2,1,0:T(8,128)(2,1)S(1)}, u32[]{:S(2)}, u32[]{:S(2)}) collective-permute-start(bf16[4,512,128]{2,1,0:T(8,128)(2,1)} %copy-done.6), channel_id=1, source_target_pairs={{0,8},{8,0},{16,24},{24,16},{32,40},{40,32},{48,56},{56,48},{64,72... | collective-permute-start | bytes 1572872 | tf_op jit(solution)/shard_map/ppermute | solution.py:50
  50.5 3.0 %collective-permute-start.16 = (bf16[4,512,128]{2,1,0:T(8,128)(2,1)}, bf16[4,512,128]{2,1,0:T(8,128)(2,1)S(1)}, u32[]{:S(2)}, u32[]{:S(2)}) collective-permute-start(bf16[4,512,128]{2,1,0:T(8,128)(2,1)} %collective-permute-done.8.refs_7_), channel_id=1, source_target_pairs={{0,8},{8,0},{16,24},{24,16},{32,40},{40,32},{48,56},{56,48},{64,72... | collective-permute-start | bytes 1572872 | tf_op jit(solution)/shard_map/ppermute | solution.py:50
  51.8 2.5 %collective-permute-start.12 = (bf16[4,512,128]{2,1,0:T(8,128)(2,1)}, bf16[4,512,128]{2,1,0:T(8,128)(2,1)S(1)}, u32[]{:S(2)}, u32[]{:S(2)}) collective-permute-start(bf16[4,512,128]{2,1,0:T(8,128)(2,1)} %collective-permute-done.5.refs_3_), channel_id=1, source_target_pairs={{0,8},{8,0},{16,24},{24,16},{32,40},{40,32},{48,56},{56,48},{64,72... | collective-permute-start | bytes 1572872 | tf_op jit(solution)/shard_map/ppermute | solution.py:50
  54.3 1.0 copy-start.3
  55.3 1.0 copy-start.5
  67.7 23.8 %all-to-all-start = ((bf16[8,64,512]{2,1,0:T(8,128)(2,1)}), bf16[8,64,512]{2,1,0:T(8,128)(2,1)S(1)}, u32[]{:S(2)}, u32[]{:S(2)}) async-start(bf16[8,64,512]{2,1,0:T(8,128)(2,1)} %attend.1.refs_2_), calls=%async_computation | async-start | bytes 1048576 | tf_op jit(solution)/shard_map/all_to_all | solution.py:312
  74.7 43.3 %copy-start.2 = (bf16[512,1024]{1,0:T(8,128)(2,1)S(1)}, bf16[512,1024]{1,0:T(8,128)(2,1)}, u32[]{:S(2)}) copy-start(bf16[512,1024]{1,0:T(8,128)(2,1)} %get-tuple-element.15.refs_11_) | copy-start | bytes 3145732
  74.7 35.9 %collective-permute-start.28 = (bf16[512,1024]{1,0:T(8,128)(2,1)}, bf16[512,1024]{1,0:T(8,128)(2,1)}, u32[]{:S(2)}, u32[]{:S(2)}) collective-permute-start(bf16[512,1024]{1,0:T(8,128)(2,1)} %get-tuple-element.15.refs_11_), channel_id=1, source_target_pairs={{0,1},{1,2},{2,3},{3,4},{4,5},{5,6},{6,7},{7,0},{8,9},{9,10},{10,1... | collective-permute-start | bytes 3145736 | tf_op jit(solution)/shard_map/ppermute | solution.py:200
  76.2 37.6 %collective-permute-start.30 = (bf16[512,1024]{1,0:T(8,128)(2,1)}, bf16[512,1024]{1,0:T(8,128)(2,1)}, u32[]{:S(2)}, u32[]{:S(2)}) collective-permute-start(bf16[512,1024]{1,0:T(8,128)(2,1)} %get-tuple-element.16.refs_12_), channel_id=1, source_target_pairs={{0,7},{1,0},{2,1},{3,2},{4,3},{5,4},{6,5},{7,6},{8,15},{9,8},{10,9... | collective-permute-start | bytes 3145736 | tf_op jit(solution)/shard_map/ppermute | solution.py:204
  91.5 26.5 %copy-start.11 = (bf16[512,1024]{1,0:T(8,128)(2,1)S(1)}, bf16[512,1024]{1,0:T(8,128)(2,1)}, u32[]{:S(2)}) copy-start(bf16[512,1024]{1,0:T(8,128)(2,1)} %copy-done.10) | copy-start | bytes 3145732
  91.5 20.5 %collective-permute-start.17 = (bf16[8,64,512]{2,1,0:T(8,128)(2,1)S(1)}, bf16[8,64,512]{2,1,0:T(8,128)(2,1)S(1)}, u32[]{:S(2)}, u32[]{:S(2)}) collective-permute-start(bf16[8,64,512]{2,1,0:T(8,128)(2,1)S(1)} %all-to-all-done.refs_0_), channel_id=1, source_target_pairs={{0,16},{8,56},{16,0},{24,40},{32,48},{40,24},{48,32},{56,8},{64,80... | collective-permute-start | bytes 1572872 | tf_op jit(solution)/shard_map/ppermute | solution.py:50
  93.5 18.6 %collective-permute-start.18 = (bf16[8,64,512]{2,1,0:T(8,128)(2,1)S(1)}, bf16[8,64,512]{2,1,0:T(8,128)(2,1)S(1)}, u32[]{:S(2)}, u32[]{:S(2)}) collective-permute-start(bf16[8,64,512]{2,1,0:T(8,128)(2,1)S(1)} %all-to-all-done.refs_0_), channel_id=1, source_target_pairs={{0,64},{8,200},{16,80},{24,216},{32,96},{40,232},{48,112},{56,248}... | collective-permute-start | bytes 1572872 | tf_op jit(solution)/shard_map/ppermute | solution.py:50
  93.5 19.1 %collective-permute-start.19 = (bf16[8,64,512]{2,1,0:T(8,128)(2,1)S(1)}, bf16[8,64,512]{2,1,0:T(8,128)(2,1)S(1)}, u32[]{:S(2)}, u32[]{:S(2)}) collective-permute-start(bf16[8,64,512]{2,1,0:T(8,128)(2,1)S(1)} %all-to-all-done.refs_0_), channel_id=1, source_target_pairs={{0,80},{8,248},{16,64},{24,232},{32,112},{40,216},{48,96},{56,200}... | collective-permute-start | bytes 1572872 | tf_op jit(solution)/shard_map/ppermute | solution.py:50
  110.6 4.3 %collective-permute-start.20 = (bf16[8,64,512]{2,1,0:T(8,128)(2,1)S(1)}, bf16[8,64,512]{2,1,0:T(8,128)(2,1)S(1)}, u32[]{:S(2)}, u32[]{:S(2)}) collective-permute-start(bf16[8,64,512]{2,1,0:T(8,128)(2,1)S(1)} %all-to-all-done.refs_0_), channel_id=1, source_target_pairs={{0,8},{8,0},{16,24},{24,16},{32,40},{40,32},{48,56},{56,48},{64,72... | collective-permute-start | bytes 1572872 | tf_op jit(solution)/shard_map/ppermute | solution.py:50
  112.0 5.9 %collective-permute-start.21 = (bf16[8,64,512]{2,1,0:T(8,128)(2,1)S(1)}, bf16[8,64,512]{2,1,0:T(8,128)(2,1)S(1)}, u32[]{:S(2)}, u32[]{:S(2)}) collective-permute-start(bf16[8,64,512]{2,1,0:T(8,128)(2,1)S(1)} %collective-permute-done.17.refs_1_), channel_id=1, source_target_pairs={{0,8},{8,0},{16,24},{24,16},{32,40},{40,32},{48,56},{56,48},{64,72... | collective-permute-start | bytes 1572872 | tf_op jit(solution)/shard_map/ppermute | solution.py:50
  112.1 5.9 %collective-permute-start.22 = (bf16[8,64,512]{2,1,0:T(8,128)(2,1)S(1)}, bf16[8,64,512]{2,1,0:T(8,128)(2,1)S(1)}, u32[]{:S(2)}, u32[]{:S(2)}) collective-permute-start(bf16[8,64,512]{2,1,0:T(8,128)(2,1)S(1)} %collective-permute-done.18.refs_2_), channel_id=1, source_target_pairs={{0,8},{8,0},{16,24},{24,16},{32,40},{40,32},{48,56},{56,48},{64,72... | collective-permute-start | bytes 1572872 | tf_op jit(solution)/shard_map/ppermute | solution.py:50
  112.6 5.4 %collective-permute-start.23 = (bf16[8,64,512]{2,1,0:T(8,128)(2,1)S(1)}, bf16[8,64,512]{2,1,0:T(8,128)(2,1)S(1)}, u32[]{:S(2)}, u32[]{:S(2)}) collective-permute-start(bf16[8,64,512]{2,1,0:T(8,128)(2,1)S(1)} %collective-permute-done.19.refs_3_), channel_id=1, source_target_pairs={{0,8},{8,0},{16,24},{24,16},{32,40},{40,32},{48,56},{56,48},{64,72... | collective-permute-start | bytes 1572872 | tf_op jit(solution)/shard_map/ppermute | solution.py:50
  113.7 14.4 %collective-permute-start.29 = (bf16[256,1024]{1,0:T(8,128)(2,1)S(1)}, bf16[256,1024]{1,0:T(8,128)(2,1)S(1)}, u32[]{:S(2)}, u32[]{:S(2)}) collective-permute-start(bf16[256,1024]{1,0:T(8,128)(2,1)S(1)} %slice.75), channel_id=1, source_target_pairs={{0,1},{1,2},{2,3},{3,4},{4,5},{5,6},{6,7},{7,0},{8,9},{9,10},{10,1... | collective-permute-start | bytes 1572872 | tf_op jit(solution)/shard_map/ppermute | solution.py:200
  114.9 13.5 %collective-permute-start.31 = (bf16[256,1024]{1,0:T(8,128)(2,1)S(1)}, bf16[256,1024]{1,0:T(8,128)(2,1)S(1)}, u32[]{:S(2)}, u32[]{:S(2)}) collective-permute-start(bf16[256,1024]{1,0:T(8,128)(2,1)S(1)} %slice.76), channel_id=1, source_target_pairs={{0,7},{1,0},{2,1},{3,2},{4,3},{5,4},{6,5},{7,6},{8,15},{9,8},{10,9... | collective-permute-start | bytes 1572872 | tf_op jit(solution)/shard_map/ppermute | solution.py:204
  129.8 6.3 %collective-permute-start.36 = (bf16[64,1024]{1,0:T(8,128)(2,1)S(1)}, bf16[64,1024]{1,0:T(8,128)(2,1)S(1)}, u32[]{:S(2)}, u32[]{:S(2)}) collective-permute-start(bf16[64,1024]{1,0:T(8,128)(2,1)S(1)} %get-tuple-element.21), channel_id=1, source_target_pairs={{0,16},{8,56},{16,0},{24,40},{32,48},{40,24},{48,32},{56,8},{64,80... | collective-permute-start | bytes 393224 | tf_op jit(solution)/shard_map/ppermute | solution.py:50
  131.9 6.9 %collective-permute-start.37 = (bf16[64,1024]{1,0:T(8,128)(2,1)S(1)}, bf16[64,1024]{1,0:T(8,128)(2,1)S(1)}, u32[]{:S(2)}, u32[]{:S(2)}) collective-permute-start(bf16[64,1024]{1,0:T(8,128)(2,1)S(1)} %get-tuple-element.22), channel_id=1, source_target_pairs={{0,56},{8,16},{16,40},{24,0},{32,24},{40,48},{48,8},{56,32},{64,12... | collective-permute-start | bytes 393224 | tf_op jit(solution)/shard_map/ppermute | solution.py:50
  133.1 6.9 %collective-permute-start.38 = (bf16[64,1024]{1,0:T(8,128)(2,1)S(1)}, bf16[64,1024]{1,0:T(8,128)(2,1)S(1)}, u32[]{:S(2)}, u32[]{:S(2)}) collective-permute-start(bf16[64,1024]{1,0:T(8,128)(2,1)S(1)} %get-tuple-element.24), channel_id=1, source_target_pairs={{0,8},{8,0},{16,24},{24,16},{32,40},{40,32},{48,56},{56,48},{64,72... | collective-permute-start | bytes 393224 | tf_op jit(solution)/shard_map/ppermute | solution.py:50
  133.1 7.2 %collective-permute-start.32 = (bf16[64,1024]{1,0:T(8,128)(2,1)S(1)}, bf16[64,1024]{1,0:T(8,128)(2,1)S(1)}, u32[]{:S(2)}, u32[]{:S(2)}) collective-permute-start(bf16[64,1024]{1,0:T(8,128)(2,1)S(1)} %get-tuple-element.17), channel_id=1, source_target_pairs={{0,80},{8,248},{16,64},{24,232},{32,112},{40,216},{48,96},{56,200}... | collective-permute-start | bytes 393224 | tf_op jit(solution)/shard_map/ppermute | solution.py:50
  134.8 7.8 %collective-permute-start.33 = (bf16[64,1024]{1,0:T(8,128)(2,1)S(1)}, bf16[64,1024]{1,0:T(8,128)(2,1)S(1)}, u32[]{:S(2)}, u32[]{:S(2)}) collective-permute-start(bf16[64,1024]{1,0:T(8,128)(2,1)S(1)} %get-tuple-element.18), channel_id=1, source_target_pairs={{0,248},{8,80},{16,232},{24,64},{32,216},{40,112},{48,200},{56,96}... | collective-permute-start | bytes 393224 | tf_op jit(solution)/shard_map/ppermute | solution.py:50
  136.2 6.9 %collective-permute-start.34 = (bf16[64,1024]{1,0:T(8,128)(2,1)S(1)}, bf16[64,1024]{1,0:T(8,128)(2,1)S(1)}, u32[]{:S(2)}, u32[]{:S(2)}) collective-permute-start(bf16[64,1024]{1,0:T(8,128)(2,1)S(1)} %get-tuple-element.19), channel_id=1, source_target_pairs={{0,64},{8,200},{16,80},{24,216},{32,96},{40,232},{48,112},{56,248}... | collective-permute-start | bytes 393224 | tf_op jit(solution)/shard_map/ppermute | solution.py:50
  138.8 5.7 %collective-permute-start.35 = (bf16[64,1024]{1,0:T(8,128)(2,1)S(1)}, bf16[64,1024]{1,0:T(8,128)(2,1)S(1)}, u32[]{:S(2)}, u32[]{:S(2)}) collective-permute-start(bf16[64,1024]{1,0:T(8,128)(2,1)S(1)} %get-tuple-element.20), channel_id=1, source_target_pairs={{0,200},{8,64},{16,216},{24,80},{32,232},{40,96},{48,248},{56,112}... | collective-permute-start | bytes 393224 | tf_op jit(solution)/shard_map/ppermute | solution.py:50
  (6 other events, 5.7 us)
